TPU v7x, 128 devices: a whole 4x4x4 slice. The times are simulated.
128 devices in a mesh: prow: 16 (over x, y), pcol: 8 (over z, core).
Axes of the slice: x: 4, y: 4, z: 4, core: 2. Of those that a mesh axis runs over, the one named last changes fastest.
Arguments:
- matrix: float32 [8, 16, 128, 16, 8, 128], P(None, 'prow', None, None, 'pcol'), may hold values from -6 to 6
- pivots: int32 [2, 128], replicated, may hold values from 0 to 16383, as said below
- block_inverses: float32 [2, 128, 128], replicated, may hold values from -0.046875 to 0.046875
Outputs:
- factored: float32 [8, 16, 128, 16, 8, 128], P(None, 'prow', None, None, 'pcol')
Inputs may be any that keep to these rules, and one draw needn't show every extreme that they name: `pivots`: entry j of step k lies in j to 16384 - k * 128 - 1.
All inputs are finite; a program needn't handle non-finite values.
Results may differ from a plain program's by a relative error of at most 0.0001.
Values sent between devices are 32-bit elements; how exact they have to be, the bound alone decides.
A program may use at most 64 MiB of HBM per device.

v0:
```python
import jax
import jax.numpy as jnp
from jax import lax
from jax.sharding import PartitionSpec as P


def broadcast(shard, axis, root):
    mine = lax.axis_index(axis) == root
    return lax.psum(jnp.where(mine, shard, jnp.zeros_like(shard)), axis)


def slot_sources(pivot_row, first_row, nblock):
    slot_list = jnp.concatenate(
        [first_row + jnp.arange(nblock, dtype=jnp.int32), first_row + pivot_row]
    )
    slot_count = 2 * nblock
    position = jnp.arange(slot_count, dtype=jnp.int32)
    matches = slot_list[:, None] == slot_list[None, :]
    canonical = jnp.min(jnp.where(matches, position[None, :], slot_count), axis=1)

    def swap_one(column, contents):
        upper_pos = canonical[column]
        lower_pos = canonical[nblock + column]
        upper_val = contents[upper_pos]
        lower_val = contents[lower_pos]
        return contents.at[upper_pos].set(lower_val).at[lower_pos].set(upper_val)

    contents = lax.fori_loop(0, nblock, swap_one, slot_list, unroll=8)
    slot_vals = contents[canonical]
    return (slot_vals[:nblock], slot_vals[nblock:])


def on_device(matrix, pivots, block_inverses):
    dims_local = matrix.shape
    nblock = dims_local[2]
    local_rows = dims_local[0] * nblock
    local_cols = dims_local[3] * nblock
    grid_rows = lax.axis_size("prow")
    grid_cols = lax.axis_size("pcol")
    row_index = lax.axis_index("prow")
    col_index = lax.axis_index("pcol")
    work_mat = matrix.reshape(local_rows, local_cols)
    row_pos = jnp.arange(local_rows, dtype=jnp.int32)
    row_global = (row_pos // nblock * grid_rows + row_index) * nblock + row_pos % nblock
    col_pos = jnp.arange(local_cols, dtype=jnp.int32)
    col_global = (col_pos // nblock * grid_cols + col_index) * nblock + col_pos % nblock
    for step_index in range(pivots.shape[0]):
        first_row = step_index * nblock
        split_at = first_row + nblock
        sources, target_src = slot_sources(pivots[step_index], first_row, nblock)
        owned_mask = sources // nblock % grid_rows == row_index
        local_src = sources // nblock // grid_rows * nblock + sources % nblock
        picked = jnp.take(work_mat, local_src, axis=0)
        contrib = jnp.where(owned_mask[:, None], picked, 0.0)
        root_row = step_index % grid_rows
        top_start = step_index // grid_rows * nblock
        old_block = work_mat[top_start : top_start + nblock]
        new_top = lax.psum(contrib, "prow")
        old_top = broadcast(old_block, "prow", root_row)
        targets = first_row + pivots[step_index]
        keep_mask = (targets >= split_at) & (targets // nblock % grid_rows == row_index)
        where_to = jnp.where(
            keep_mask, targets // nblock // grid_rows * nblock + targets % nblock, local_rows
        )
        values = jnp.take(old_top, jnp.clip(target_src - first_row, 0, nblock - 1), axis=0)
        work_mat = work_mat.at[top_start : top_start + nblock].set(
            jnp.where(row_index == root_row, new_top, old_block)
        )
        work_mat = work_mat.at[where_to].set(values, mode="drop")
        root_col = step_index % grid_cols
        col_start = step_index // grid_cols * nblock
        panel_cols = work_mat[:, col_start : col_start + nblock]
        below_mask = (row_global >= split_at)[:, None]
        lower_panel = jnp.where(below_mask, panel_cols, 0.0)
        inverse = block_inverses[step_index]
        own_factor = jnp.dot(
            lower_panel,
            inverse,
            precision=lax.Precision.HIGHEST,
            preferred_element_type=jnp.float32,
        )
        factor = broadcast(own_factor, "pcol", root_col)
        stored = jnp.where((col_index == root_col) & below_mask, factor, panel_cols)
        work_mat = work_mat.at[:, col_start : col_start + nblock].set(stored)
        upper_rows = jnp.where((col_global >= split_at)[None, :], new_top, 0.0)
        work_mat = work_mat - jnp.dot(
            factor, upper_rows, precision=lax.Precision.HIGHEST, preferred_element_type=jnp.float32
        )
    return work_mat.reshape(dims_local)


def solution(mesh):
    in_specs = (P(None, "prow", None, None, "pcol", None), P(), P())
    out_specs = P(None, "prow", None, None, "pcol", None)
    return jax.shard_map(
        on_device, mesh=mesh, in_specs=in_specs, out_specs=out_specs, check_vma=False
    )
```

profile of v0, /device:TPU:65, one launch (start us, length us, event | category | flops | bytes accessed | tf_op | source)
XLA Modules:
  0.0 1866.9 jit_solution(4226074193581712750)
XLA Ops:
  7.7 774.5 %while.74 = (s32[]{:T(128)}, s32[256]{0:T(256)S(1)}, s32[256]{0:T(256)S(1)}, s32[]{:T(128)}, s32[]{:T(128)}, /*index=5*/s32[]{:T(128)}, s32[]{:T(128)}, s32[]{:T...) while((s32[]{:T(128)}, s32[256]{0:T(256)S(1)}, ...), condition=%wide.region_2.3_spmd.clone.clone, body=%wide.region_1.2_spmd.clone.clone.clone.sunk | while | flops 178 | bytes 18781 | solution.py:28
  782.2 2.1 gather_fusion
  784.4 4.0 slice_reduce_fusion
  788.4 10.9 copy.13
  799.3 4.8 gather_fusion.2
  804.2 1.4 bitcast_select_fusion
  805.6 1.2 select_select_fusion.1
  806.9 773.2 %while.75 = (s32[]{:T(128)}, s32[256]{0:T(256)S(1)}, s32[256]{0:T(256)S(1)}, s32[]{:T(128)}, s32[]{:T(128)}, /*index=5*/s32[]{:T(128)}, s32[]{:T(128)}, s32[]{:T...) while((s32[]{:T(128)}, s32[256]{0:T(256)S(1)}, ...), condition=%wide.region_10.13_spmd.clone.clone, body=%wide.region_9.12_spmd.clone.clone.clone.sunk | while | flops 178 | bytes 18781 | solution.py:28
  840.6 0.9 select_dynamic-update-slice_fusion.83
  841.5 0.9 select_dynamic-update-slice_fusion.84
  888.9 0.9 select_dynamic-update-slice_fusion.83
  889.8 0.9 select_dynamic-update-slice_fusion.84
  937.2 0.9 select_dynamic-update-slice_fusion.83
  938.1 0.9 select_dynamic-update-slice_fusion.84
  985.5 0.9 select_dynamic-update-slice_fusion.83
  986.4 0.9 select_dynamic-update-slice_fusion.84
  1033.8 0.9 select_dynamic-update-slice_fusion.83
  1034.7 0.9 select_dynamic-update-slice_fusion.84
  1082.1 0.9 select_dynamic-update-slice_fusion.83
  1083.0 0.9 select_dynamic-update-slice_fusion.84
  1130.4 0.9 select_dynamic-update-slice_fusion.83
  1131.3 0.9 select_dynamic-update-slice_fusion.84
  1178.7 0.9 select_dynamic-update-slice_fusion.83
  1179.6 0.9 select_dynamic-update-slice_fusion.84
  1227.0 0.9 select_dynamic-update-slice_fusion.83
  1227.9 0.9 select_dynamic-update-slice_fusion.84
  1323.6 0.9 select_dynamic-update-slice_fusion.83
  1372.8 0.9 select_dynamic-update-slice_fusion.84
  1468.5 0.9 select_dynamic-update-slice_fusion.83
  1517.7 0.9 select_dynamic-update-slice_fusion.84
  1580.0 1.9 gather_fusion.1
  1582.2 2.8 fusion
  1584.9 10.2 scatter_custom_fusion
  1595.1 2.4 convolution_select_fusion.1
  1598.3 57.2 %all-reduce.7.cloned.1.call-done = f32[1024,128]{1,0:T(8,128)} async-done(((f32[1024,128]{1,0:T(8,128)}), f32[1024,128]{1,0:T(8,128)}) %all-reduce.7.cloned.1.call-update) | async-done | bytes 524304 | tf_op jit(solution)/shard_map/psum | solution.py:9
  1655.5 2.8 fusion.7
  1658.3 11.2 convolution_subtract_fusion
  1669.5 4.8 gather_fusion.3
  1674.3 2.3 slice_select_fusion
  1676.6 1.2 select_select_fusion
  1678.2 91.4 %all-reduce.11.cloned.1.call-done = (f32[128,2048]{1,0:T(8,128)}, f32[128,2048]{1,0:T(8,128)}) async-done(((f32[128,2048]{1,0:T(8,128)}, f32[128,2048]{1,0:T(8,128)}), (f32[128,2048]{1,0:T(8,128)}, f32[128,2048]{1,0:T(8,128)})) %all-reduce.11.cloned.1.call-update) | async-done | bytes 2097168 | tf_op jit(solution)/shard_map/psum | solution.py:58
  1769.6 2.4 select_dynamic-update-slice_fusion.32
  1772.1 10.2 scatter_custom_fusion.1
  1782.2 2.5 convolution_select_fusion
  1784.7 58.2 %all-reduce.9.cloned.1.call-done = f32[1024,128]{1,0:T(8,128)} async-done(((f32[1024,128]{1,0:T(8,128)}), f32[1024,128]{1,0:T(8,128)}) %all-reduce.9.cloned.1.call-update) | async-done | bytes 524304 | tf_op jit(solution)/shard_map/psum | solution.py:9
  1842.9 2.8 fusion.8
  1845.7 9.2 subtract_bitcast_fusion
  1854.9 5.4 copy.9
  (821 shorter events, 576.9 us)
Async XLA Ops:
  6.5 1575.6 %all-reduce.13.cloned.1.call-start = ((), (), s32[]{:S(2)}) async-start(), calls=%async_computation.3 | async-start | bytes 4194304 | tf_op jit(solution)/shard_map/psum | solution.py:58
  799.3 782.7 %copy-start.3 = (s32[2,128]{1,0:T(2,128)S(1)}, s32[2,128]{1,0:T(2,128)}, u32[]{:S(2)}) copy-start(s32[2,128]{1,0:T(2,128)} %param.84) | copy-start | bytes 3076
  806.8 848.7 %all-reduce.7.cloned.1.call-start = ((), (), s32[]{:S(2)}) async-start(), calls=%async_computation | async-start | bytes 1048576 | tf_op jit(solution)/shard_map/psum | solution.py:9
  806.9 788.2 %copy-start.2 = (f32[2,128,128]{2,1,0:T(8,128)S(1)}, f32[2,128,128]{2,1,0:T(8,128)}, u32[]{:S(2)}) copy-start(f32[2,128,128]{2,1,0:T(8,128)} %param.85) | copy-start | bytes 393220
  1582.1 76.1 %copy-start = (f32[128,2048]{1,0:T(8,128)S(1)}, f32[128,2048]{1,0:T(8,128)}, u32[]{:S(2)}) copy-start(f32[128,2048]{1,0:T(8,128)} %get-tuple-element.865) | copy-start | bytes 3145732
  1597.6 172.1 %all-reduce.11.cloned.1.call-start = ((), (), s32[]{:S(2)}) async-start(), calls=%async_computation.2 | async-start | bytes 4194304 | tf_op jit(solution)/shard_map/psum | solution.py:58
  1677.8 165.1 %all-reduce.9.cloned.1.call-start = ((), (), s32[]{:S(2)}) async-start(), calls=%async_computation.1 | async-start | bytes 1048576 | tf_op jit(solution)/shard_map/psum | solution.py:9
  1769.6 76.1 %copy-start.1 = (f32[128,2048]{1,0:T(8,128)S(1)}, f32[128,2048]{1,0:T(8,128)}, u32[]{:S(2)}) copy-start(f32[128,2048]{1,0:T(8,128)} %get-tuple-element.863) | copy-start | bytes 3145732
Sparse Core Ops, SparseCore 0:
  806.9 90.9 all-reduce.12
  1597.7 57.7 all-reduce.6
  1678.0 91.6 all-reduce.10
  1784.8 58.0 all-reduce.8
where the time goes:
time: 1890 us; the launch traced here: 1870 us
  loops' own time  954 us (50%)
  other arithmetic  450 us (24%)
  local copies, waits for them, and re-layouts  217 us (11%)
  waiting for transfers between devices  207 us (11%)
  matrix products  25.3 us (1%)
    another operation x2, loops' own time, slot_sources(): contents = lax.fori_loop(0, nblock, swap_one, slot_list, unroll=8)  954 us
    scatter x512, other arithmetic, swap_one(): return contents.at[upper_pos].set(lower_val).at[lower_pos].set(upper_val)  411 us
    another operation x256, local copies, waits for them, and re-layouts  159 us
    psum x2, waiting for transfers between devices, broadcast(): return lax.psum(jnp.where(mine, shard, jnp.zeros_like(shard)), axis)  115 us
    psum x2, waiting for transfers between devices, on_device(): new_top = lax.psum(contrib, 'prow')  91.5 us
  transfers between devices with their start and end apart: 4, of which 3 were waited for; matrix products, arithmetic and copies ran while one was open for 16% of the time, Pallas kernels for 0%

commit v1 on v0

v1 whole, which is shorter than its diff:
```python
import functools

import jax
import jax.numpy as jnp
from jax import lax
from jax.experimental import pallas as pl
from jax.experimental.pallas import tpu as pltpu
from jax.sharding import PartitionSpec as P

MESH = pl.DeviceIdType.MESH
NB = 128
NT = 256
DEV = 16
ROWS = 1024
FEW = 2
MANY = 16
MIB = 1 << 20

T_PLACE, T_DST, T_SRC, T_COUNT, T_PICK_FEW, T_PICK_MANY, T_SEND_MANY, T_MOST = range(8)


def iota(shape, dim):
    return lax.broadcasted_iota(jnp.int32, shape, dim)


def fiota(shape, dim):
    return iota(shape, dim).astype(jnp.float32)


def plan_kernel(piv_ref, a_ref, table_ref, send_ref, row_buf, row_smem, sem, row_sem):
    me = lax.axis_index("prow")
    sq = (NT, NT)
    sub, lane = fiota(sq, 0), fiota(sq, 1)
    diag = sub == lane
    lane1 = fiota((1, NT), 1)

    def to_col(row):
        return jnp.sum(jnp.where(diag, row, 0.0), axis=1, keepdims=True)

    piv = piv_ref[...].astype(jnp.float32)
    t_row = jnp.concatenate([piv[0:1, :], piv[1:2, :] + float(NB)], axis=1)
    t_col = to_col(t_row)
    before = sub < lane
    same = t_col == t_row
    last_same = jnp.max(jnp.where(same & before, sub, -1.0), axis=0, keepdims=True)
    later = jnp.max(jnp.where(same & (sub > lane), 1.0, 0.0), axis=0, keepdims=True)
    parent = jnp.max(jnp.where((t_col == lane) & before, sub, -1.0), axis=0, keepdims=True)
    c_row = jnp.where(parent < 0.0, lane1, parent)

    def jump(_, c_row):
        c_col = to_col(c_row)
        return jnp.sum(jnp.where(sub == c_row, c_col, 0.0), axis=0, keepdims=True)

    c_row = lax.fori_loop(0, 8, jump, c_row)
    c_col = to_col(c_row)
    from_swap = jnp.sum(jnp.where(sub == last_same, c_col, 0.0), axis=0, keepdims=True)
    src = jnp.where(last_same < 0.0, t_row, from_swap).astype(jnp.int32)
    owner = (src >> 7) & (DEV - 1)
    local = ((src >> 11) << 7) + (src & (NB - 1))
    owner_row = owner.astype(jnp.float32)
    owner_col = to_col(owner_row)
    less = owner_col < owner_row
    first = jnp.sum(jnp.where(less, 1.0, 0.0), axis=0, keepdims=True).astype(jnp.int32)
    ahead = less | ((owner_col == owner_row) & before)
    pos = jnp.sum(jnp.where(ahead, 1.0, 0.0), axis=0, keepdims=True).astype(jnp.int32)
    rank = pos - first
    most = jnp.max(rank.astype(jnp.float32), axis=1, keepdims=True) + 1.0
    bin_ = pos & (DEV - 1)
    place = bin_ * 16 + (pos >> 4)
    table_ref[T_PLACE : T_PLACE + 1, :] = place
    table_ref[T_MOST : T_MOST + 1, :] = jnp.broadcast_to(most, (1, NT)).astype(jnp.int32)

    mine = owner == me
    local_col = to_col(local.astype(jnp.float32))
    which = rank >> 4
    few = to_col(jnp.where(mine, bin_ * FEW + which, -1).astype(jnp.float32))
    send_few = jnp.sum(jnp.where(few == lane, local_col, 0.0), axis=0, keepdims=True)
    row_buf[0:1, :] = send_few.astype(jnp.int32)
    to_smem = pltpu.make_async_copy(row_buf, row_smem, sem)
    to_smem.start()

    many = to_col(jnp.where(mine, bin_ * MANY + which, -1).astype(jnp.float32))
    send_many = jnp.sum(jnp.where(many == lane, local_col, 0.0), axis=0, keepdims=True)
    table_ref[T_SEND_MANY : T_SEND_MANY + 1, :] = send_many.astype(jnp.int32)

    my_slot = to_col(jnp.where(bin_ == me, pos >> 4, -1).astype(jnp.float32)) == lane
    for row, k in ((T_PICK_FEW, FEW), (T_PICK_MANY, MANY)):
        from_col = to_col((owner * k + which).astype(jnp.float32))
        pick = jnp.sum(jnp.where(my_slot, from_col, 0.0), axis=0, keepdims=True)
        table_ref[row : row + 1, :] = pick.astype(jnp.int32)

    target = t_row.astype(jnp.int32)
    kept = (later < 0.5) & (target >= NT) & (((target >> 7) & (DEV - 1)) == me)
    dst = ((target >> 11) << 7) + (target & (NB - 1))
    c = c_row.astype(jnp.int32)
    within = c & (NB - 1)
    old = NT + (within >> 3) * 16 + (c >> 7) * 8 + (within & 7)
    kept_col = to_col(jnp.where(kept, 1.0, 0.0))
    order = jnp.sum(jnp.where(before & (kept_col > 0.5), 1.0, 0.0), axis=0, keepdims=True)
    slot = to_col(jnp.where(kept, order, -1.0)) == lane
    for row, value in ((T_DST, dst), (T_SRC, old)):
        col = to_col(value.astype(jnp.float32))
        out = jnp.sum(jnp.where(slot, col, 0.0), axis=0, keepdims=True)
        table_ref[row : row + 1, :] = out.astype(jnp.int32)
    count = jnp.sum(jnp.where(kept, 1.0, 0.0), axis=1, keepdims=True)
    table_ref[T_COUNT : T_COUNT + 1, :] = jnp.broadcast_to(count, (1, NT)).astype(jnp.int32)

    to_smem.wait()
    copies = [
        pltpu.make_async_copy(a_ref.at[row_smem[0, i]], send_ref.at[i], row_sem.at[i])
        for i in range(DEV * FEW)
    ]
    for copy in copies:
        copy.start()
    for copy in copies:
        copy.wait()


def plan(pivots, work):
    return pl.pallas_call(
        plan_kernel,
        out_shape=(
            jax.ShapeDtypeStruct((8, NT), jnp.int32),
            jax.ShapeDtypeStruct((DEV * FEW, DEV, NB), jnp.float32),
        ),
        in_specs=[pl.BlockSpec(memory_space=pltpu.VMEM), pl.BlockSpec(memory_space=pl.ANY)],
        out_specs=(pl.BlockSpec(memory_space=pltpu.VMEM), pl.BlockSpec(memory_space=pl.ANY)),
        scratch_shapes=[
            pltpu.VMEM((8, NT), jnp.int32),
            pltpu.SMEM((8, NT), jnp.int32),
            pltpu.SemaphoreType.DMA,
            pltpu.SemaphoreType.DMA((DEV * FEW,)),
        ],
        name="plan",
    )(pivots, work)


def move_kernel(
    k, table_ref, send_ref, a_ref,
    new_out, old_out, panel_out, top_out,
    got, new, old, panel, top,
    s_got, r_got, s_scat, r_scat, s_ag, r_ag, s_z, r_z, s_sib, r_sib, s_loc,
):
    me = lax.axis_index("prow")
    col = lax.axis_index("pcol")
    x, y = me // 4, me % 4
    z, core = col // 2, col % 2
    sends = []

    def at(px, py):
        return (lax.rem(px + 4, 4) * 4 + lax.rem(py + 4, 4), col)

    def remote(src, dst, send_sem, recv_sem, device):
        return pltpu.make_async_remote_copy(
            src_ref=src, dst_ref=dst, send_sem=send_sem, recv_sem=recv_sem,
            device_id=device, device_id_type=MESH,
        )

    offsets = [(dx, dy) for dx in range(4) for dy in range(4) if (dx, dy) != (0, 0)]
    sibling = (me, z * 2 + 1 - core)
    up = (me, lax.rem(z + 1, 4) * 2 + core)
    down = (me, lax.rem(z + 3, 4) * 2 + core)

    mine = pltpu.make_async_copy(a_ref.at[:, 0, :], panel.at[core], s_loc.at[0])
    on_root = z == 0

    @pl.when(on_root)
    def _():
        mine.start()

    barrier = pltpu.get_barrier_semaphore()
    for dx, dy in offsets:
        pl.semaphore_signal(barrier, inc=1, device_id=at(x + dx, y + dy), device_id_type=MESH)
    for device in (sibling, up, down):
        pl.semaphore_signal(barrier, inc=1, device_id=device, device_id_type=MESH)
    pl.semaphore_wait(barrier, len(offsets) + 3)

    for j, (dx, dy) in enumerate(offsets):
        device = at(x + dx, y + dy)
        copy = remote(
            send_ref.at[pl.ds(device[0] * k, k)], got.at[pl.ds(me * k, k)],
            s_got.at[j], r_got.at[j], device,
        )
        copy.start()
        sends.append(copy)
    own = pltpu.make_async_copy(
        send_ref.at[pl.ds(me * k, k)], got.at[pl.ds(me * k, k)], s_loc.at[1]
    )
    own.start()

    def scatter(half):
        copies = []
        for j, (dx, dy) in enumerate(offsets):
            device = at(x + dx, y + dy)
            copies.append(
                remote(
                    a_ref.at[pl.ds(device[0] * 8, 8)],
                    old.at[pl.ds(device[0] * 16 + half * 8, 8)],
                    s_scat.at[j], r_scat.at[half], device,
                )
            )
        return copies

    def scatter_own(half):
        return pltpu.make_async_copy(
            a_ref.at[pl.ds(me * 8, 8)], old.at[pl.ds(me * 16 + half * 8, 8)], s_loc.at[2]
        )

    for half in range(2):

        @pl.when(me == half)
        def _():
            for copy in scatter(half):
                copy.start()
            scatter_own(half).start()

    stage = jnp.where(core == 0, z, lax.rem(4 - z, 4))
    onward = (me, jnp.where(core == 0, lax.rem(z + 1, 4), lax.rem(z + 3, 4)) * 2 + core)
    parts = 4
    size = ROWS // parts

    panel_pieces = []
    for i in range(parts):
        ref = panel.at[core, pl.ds(i * size, size)]
        other = panel.at[1 - core, pl.ds(i * size, size)]
        panel_pieces.append((ref, other, i))
    top_pieces = []
    for i in range(2):
        top_pieces.append((top.at[i, core], top.at[i, 1 - core], parts + i))

    def z_onward(piece):
        ref, _, n = piece
        return remote(ref, ref, s_z.at[n], r_z.at[n], onward)

    def z_sibling(piece):
        ref, _, n = piece
        return remote(ref, ref, s_sib.at[n], r_sib.at[n], sibling)

    def z_step(piece):
        @pl.when(z > 0)
        def _():
            z_onward(piece).wait_recv()

        @pl.when(stage < 3)
        def _():
            z_onward(piece).start()

        z_sibling(piece).start()

    def z_finish(piece):
        ref, other, n = piece

        @pl.when(stage < 3)
        def _():
            z_onward(piece).wait_send()

        z_sibling(piece).wait_send()
        remote(other, other, s_sib.at[n], r_sib.at[n], sibling).wait_recv()

    @pl.when(on_root)
    def _():
        mine.wait()
        for piece in panel_pieces:
            z_onward(piece).start()
            z_sibling(piece).start()

    def ring(axis, step):
        if axis == 0:
            return lax.rem(x + step + 4, 4) * 4 + y
        return x * 4 + lax.rem(y + step + 4, 4)

    def shifted(index, axis, step):
        px, py = index // 4, index % 4
        if axis == 0:
            return lax.rem(px + step + 4, 4) * 4 + py
        return px * 4 + lax.rem(py + step + 4, 4)

    def piece(buf, index, half, part=None):
        if part is None:
            return buf.at[pl.ds(index * 16, 16), pl.ds(half * 8, 8)]
        return buf.at[pl.ds(index * 16 + part * 8, 8), pl.ds(half * 8, 8)]

    class Gather:
        def __init__(self, buf, half, base):
            self.buf, self.half, self.base = buf, half, base
            self.axes = (0, 1) if half == 0 else (1, 0)

        def sem(self, phase, item, role):
            return self.base + phase * (1 + item) * 4 + role

        def start_own(self, phase, item, index):
            axis = self.axes[phase]
            for role, step in ((0, 1), (1, 3)):
                n = self.sem(phase, item, role)
                ref = piece(self.buf, index, self.half)
                copy = remote(ref, ref, s_ag.at[n], r_ag.at[n], (ring(axis, step), col))
                copy.start()
                sends.append(copy)

        def wait_near(self, phase, item, index, role):
            axis = self.axes[phase]
            n = self.sem(phase, item, role)
            came = shifted(index, axis, 3 if role == 0 else 1)
            ref = piece(self.buf, came, self.half)
            remote(ref, ref, s_ag.at[n], r_ag.at[n], (ring(axis, 1), col)).wait_recv()
            n = self.sem(phase, item, 2 + role)
            ref = piece(self.buf, came, self.half, role)
            copy = remote(
                ref, ref, s_ag.at[n], r_ag.at[n], (ring(axis, 1 if role == 0 else 3), col)
            )
            copy.start()
            sends.append(copy)
            return came

        def wait_far(self, phase, item, index):
            axis = self.axes[phase]
            came = shifted(index, axis, 2)
            for role in range(2):
                n = self.sem(phase, item, 2 + role)
                ref = piece(self.buf, came, self.half, role)
                remote(ref, ref, s_ag.at[n], r_ag.at[n], (ring(axis, 1), col)).wait_recv()
            return came

    per = 5 * 4

    def gather(buf, base):
        halves = [Gather(buf, h, base + h * per) for h in range(2)]
        for g in halves:
            g.start_own(0, 0, me)
            g.start_own(1, 0, me)
        items = [[me], [me]]
        for role in range(2):
            for h, g in enumerate(halves):
                came = g.wait_near(0, 0, me, role)
                g.start_own(1, 1 + role, came)
                items[h].append(came)
        for h, g in enumerate(halves):
            came = g.wait_far(0, 0, me)
            g.start_own(1, 3, came)
            items[h].append(came)
        for i in range(4):
            for h, g in enumerate(halves):
                for role in range(2):
                    g.wait_near(1, i, items[h][i], role)
        for i in range(4):
            for h, g in enumerate(halves):
                g.wait_far(1, i, items[h][i])

    for j, (dx, dy) in enumerate(offsets):
        sender = at(x - dx, y - dy)[0]
        remote(
            send_ref.at[pl.ds(0, k)], got.at[pl.ds(sender * k, k)],
            s_got.at[j], r_got.at[j], at(x + dx, y + dy),
        ).wait_recv()
    own.wait()
    pick_row = T_PICK_FEW if k == FEW else T_PICK_MANY
    for s in range(16):
        new[me * 16 + s] = got[table_ref[pick_row, s]]

    for half in range(2):
        part = old.at[pl.ds(me * 16 + half * 8, 8)]

        @pl.when(me == half)
        def _():
            scatter_own(half).wait()
            for copy in scatter(half):
                copy.wait_send()

        @pl.when(me != half)
        def _():
            remote(
                a_ref.at[pl.ds(0, 8)], part, s_scat.at[0], r_scat.at[half], at(x + 1, y)
            ).wait_recv()

    gather(new, 0)

    @pl.when(z > 0)
    def _():
        for p in panel_pieces:
            z_step(p)

    gather(old, 2 * per)

    @pl.when(on_root)
    def _():
        for i, buf in enumerate((new, old)):
            top[i, core] = buf.reshape(NT * DEV, NB)[pl.ds(0, NT, stride=DEV), :]

    for p in top_pieces:
        z_step(p)
    for p in panel_pieces + top_pieces:
        z_finish(p)
    outs = [
        pltpu.make_async_copy(a, b, s_loc.at[3 + i])
        for i, (a, b) in enumerate(
            ((new, new_out), (old, old_out), (panel, panel_out), (top, top_out))
        )
    ]
    for copy in outs:
        copy.start()
    for copy in sends:
        copy.wait_send()
    for copy in outs:
        copy.wait()


def move(k, table, send, work):
    shapes = (
        (NT, DEV, NB),
        (NT, DEV, NB),
        (2, ROWS, NB),
        (2, 2, NT, NB),
    )
    dma = pltpu.SemaphoreType.DMA
    ag = 4 * 20
    return pl.pallas_call(
        functools.partial(move_kernel, k),
        out_shape=tuple(jax.ShapeDtypeStruct(s, jnp.float32) for s in shapes),
        in_specs=[
            pl.BlockSpec(memory_space=pltpu.SMEM),
            pl.BlockSpec(memory_space=pl.ANY),
            pl.BlockSpec(memory_space=pl.ANY),
        ],
        out_specs=tuple(pl.BlockSpec(memory_space=pl.ANY) for _ in shapes),
        scratch_shapes=[pltpu.VMEM((DEV * k, DEV, NB), jnp.float32)]
        + [pltpu.VMEM(s, jnp.float32) for s in shapes]
        + [
            dma((15,)), dma((15,)), dma((15,)), dma((2,)), dma((ag,)), dma((ag,)),
            dma((6,)), dma((6,)), dma((6,)), dma((6,)), dma((7,)),
        ],
        compiler_params=pltpu.CompilerParams(
            collective_id=k, has_side_effects=True, vmem_limit_bytes=24 * MIB
        ),
        name=f"move_{k}",
    )(table, send, work)


def split(a):
    hi = a.astype(jnp.bfloat16)
    return hi, (a - hi.astype(jnp.float32)).astype(jnp.bfloat16)


def dot(a, b):
    return jnp.dot(a, b, preferred_element_type=jnp.float32)


def dot3(a, b):
    return dot(a[0], b[0]) + (dot(a[0], b[1]) + dot(a[1], b[0]))


CHUNKS = 4
CROWS = ROWS // CHUNKS


def update_kernel(
    table_ref, inv_ref, place_ref, a_ref, new_ref, old_ref, panel_ref, top_ref,
    out_ref,
    a, rows, panel, top, b_hi, b_lo, g_hi, g_lo, sems,
):
    me = lax.axis_index("prow")
    col = lax.axis_index("pcol")
    loads = [
        pltpu.make_async_copy(panel_ref, panel, sems.at[0]),
        pltpu.make_async_copy(top_ref, top, sems.at[1]),
        pltpu.make_async_copy(new_ref, rows.at[pl.ds(0, NT)], sems.at[2]),
        pltpu.make_async_copy(old_ref, rows.at[pl.ds(NT, NT)], sems.at[3]),
    ]
    a_loads = [
        pltpu.make_async_copy(
            a_ref.at[pl.ds(i * CROWS, CROWS)], a.at[pl.ds(i * CROWS, CROWS)], sems.at[4 + i]
        )
        for i in range(CHUNKS)
    ]
    for copy in loads + a_loads:
        copy.start()
    loads[0].wait()
    loads[1].wait()

    count = table_ref[T_COUNT, 0]

    def fix_panel(dst, src):
        kind, row = src // NT, lax.rem(src, NT)
        for p in range(2):
            panel[p, pl.ds(dst, 1), :] = top[kind, p, pl.ds(row, 1), :]

    def fix_row(dst, src):
        a[dst] = rows[src]

    def fix_all(fix):
        @pl.when(me < 2)
        def _():
            @pl.loop(0, NB)
            def _(i):
                fix(i, table_ref[T_PLACE, me * NB + i])

        @pl.loop(0, count)
        def _(i):
            fix(table_ref[T_DST, i], table_ref[T_SRC, i])

    fix_all(fix_panel)

    place = place_ref[T_PLACE : T_PLACE + 1, :]
    order_t = jnp.where(iota((NT, NT), 0) == place, 1.0, 0.0).astype(jnp.bfloat16)

    def pick(lo, val):
        return lax.dot_general(
            order_t[:, lo : lo + NB], val, (((0,), (0,)), ((), ())),
            preferred_element_type=jnp.float32,
        )

    inv = [split(inv_ref[s]) for s in range(2)]
    u_split = split(top[0, 1])
    u0p = tuple(pick(0, v).astype(jnp.bfloat16) for v in u_split)
    p_split = split(top[0, 0])
    l0b = dot3(tuple(pick(NB, v).astype(jnp.bfloat16) for v in p_split), inv[0])
    l0b = split(l0b)

    for i in range(CHUNKS):
        part = pl.ds(i * CROWS, CROWS)
        l0 = dot3(split(panel[0, part, :]), inv[0])
        if i == 0:
            top_rows = iota((CROWS, NB), 0) < NB
            l0 = jnp.where(top_rows & (me == 0), 0.0, l0)
        rest = panel[1, part, :] - dot3(split(l0), u0p)
        l1 = dot3(split(rest), inv[1])
        if i == 0:
            l1 = jnp.where(top_rows & (me < 2), 0.0, l1)
        g0 = l0 - dot3(split(l1), l0b)
        panel[0, part, :] = l0
        panel[1, part, :] = l1
        g = split(jnp.concatenate([g0, l1], axis=1))
        for ref, val in ((g_hi, g[0]), (g_lo, g[1])):
            ref[part, :] = lax.dot_general(
                val, order_t, (((1,), (1,)), ((), ())), preferred_element_type=jnp.float32
            ).astype(jnp.bfloat16)

    for copy in loads[2:]:
        copy.wait()
    flat = rows.reshape(2 * NT * DEV, NB)
    for c in range(DEV):
        hi, lo = split(flat[pl.ds(c, NT, stride=DEV), :])
        b_hi[:, c * NB : (c + 1) * NB] = hi
        b_lo[:, c * NB : (c + 1) * NB] = lo
    for copy in a_loads:
        copy.wait()
    fix_all(fix_row)

    aflat = a.reshape(ROWS * DEV, NB)
    stores = []
    for i in range(CHUNKS):
        part = pl.ds(i * CROWS, CROWS)

        for c in range(0, DEV, 2):
            wide = slice(c * NB, (c + 2) * NB)
            upd = dot3((g_hi[part, :], g_lo[part, :]), (b_hi[:, wide], b_lo[:, wide]))
            for h in range(2):
                where = pl.ds(i * CROWS * DEV + c + h, CROWS, stride=DEV)
                base = aflat[where, :]
                val = base - upd[:, h * NB : (h + 1) * NB]
                if c + h == 0:
                    fac = jnp.where(col == 0, panel[0, part, :], panel[1, part, :])
                    if i == 0:
                        top_rows = iota((CROWS, NB), 0) < NB
                        keep = jnp.where(col == 0, me == 0, me < 2)
                        same = top_rows & keep
                        base_or = jnp.where(col == 0, base, val)
                        fac = jnp.where(same, base_or, fac)
                    val = jnp.where(col < 2, fac, val)
                aflat[where, :] = val
        store = pltpu.make_async_copy(a.at[part], out_ref.at[part], sems.at[4 + i])
        store.start()
        stores.append(store)
    for store in stores:
        store.wait()


def update(table, inverses, work, new, old, panel, top):
    any_ = pl.BlockSpec(memory_space=pl.ANY)
    return pl.pallas_call(
        update_kernel,
        out_shape=jax.ShapeDtypeStruct((ROWS, DEV, NB), jnp.float32),
        in_specs=[
            pl.BlockSpec(memory_space=pltpu.SMEM),
            pl.BlockSpec(memory_space=pltpu.VMEM),
            pl.BlockSpec(memory_space=pltpu.VMEM),
            any_, any_, any_, any_, any_,
        ],
        out_specs=any_,
        scratch_shapes=[
            pltpu.VMEM((ROWS, DEV, NB), jnp.float32),
            pltpu.VMEM((2 * NT, DEV, NB), jnp.float32),
            pltpu.VMEM((2, ROWS, NB), jnp.float32),
            pltpu.VMEM((2, 2, NT, NB), jnp.float32),
            pltpu.VMEM((NT, DEV * NB), jnp.bfloat16),
            pltpu.VMEM((NT, DEV * NB), jnp.bfloat16),
            pltpu.VMEM((ROWS, NT), jnp.bfloat16),
            pltpu.VMEM((ROWS, NT), jnp.bfloat16),
            pltpu.SemaphoreType.DMA((4 + CHUNKS,)),
        ],
        compiler_params=pltpu.CompilerParams(vmem_limit_bytes=40 * MIB),
        name="update",
    )(table, inverses, table, work, new, old, panel, top)


def on_device(matrix, pivots, block_inverses):
    work = matrix.reshape(ROWS, DEV, NB)
    table, send = plan(pivots, work)

    def few():
        return move(FEW, table, send, work)

    def many():
        rows = jnp.take(work, table[T_SEND_MANY], axis=0)
        return move(MANY, table, rows, work)

    moved = lax.cond(table[T_MOST, 0] <= FEW * DEV, few, many)
    out = update(table, block_inverses, work, *moved)
    return out.reshape(matrix.shape)


def solution(mesh):
    in_specs = (P(None, "prow", None, None, "pcol", None), P(), P())
    out_specs = P(None, "prow", None, None, "pcol", None)
    return jax.shard_map(
        on_device, mesh=mesh, in_specs=in_specs, out_specs=out_specs, check_vma=False
    )
```

time: 1890 us -> 97.1 us (0.05)
  the two profiles are of different devices: /device:TPU:65 before, /device:TPU:97 now
where the time goes in v1:
time: 97.1 us; the launch traced here: 96.9 us
  Pallas kernels  95.5 us (98%)
    pallas_call x1, Pallas kernels, move(): pl.pallas_call(functools.partial(move_kernel, k), out_shape=tuple((jax.Sh...  73.4 us
    pallas_call x1, Pallas kernels, update(): pl.pallas_call(update_kernel, out_shape=jax.ShapeDtypeStruct((ROWS, DEV,...  17.6 us
    pallas_call x1, Pallas kernels, plan(): pl.pallas_call(plan_kernel, out_shape=(jax.ShapeDtypeStruct((8, NT), jnp....  4.46 us

profile of v1, /device:TPU:97, one launch (start us, length us, event | category | flops | bytes accessed | tf_op | source)
XLA Modules:
  0.0 96.9 jit_solution(15924665007184196732)
XLA Ops:
  0.0 4.5 %plan.1 = (s32[8,256]{1,0:T(8,128)S(1)}, f32[32,16,128]{2,1,0:T(8,128)S(1)}) custom-call(s32[2,128]{1,0:T(2,128)} %piv_ref.1, f32[1024,16,128]{2,1,0:T(8,128)} %bitcast.9), custom_call_target="tpu_custom_call" | custom-call | tf_op jit(solution)/shard_map/plan/pallas_call | solution.py:120
  4.5 0.5 slice.6
  5.6 0.0 copy-start
  5.6 73.4 %conditional.1 = ((f32[256,16,128]{2,1,0:T(8,128)S(1)}, f32[256,16,128]{2,1,0:T(8,128)}, f32[2,1024,128]{2,1,0:T(8,128)S(1)}, f32[2,2,256,128]{3,2,1,0:T(8,128)})) conditional(s32[]{:T(128)} %bitcast.4, (s32[8,256]{1,0:T(8,128)S(1)}, f32[1024,16,128]{2,1,0:T(8,128)}) %tuple.17, (s32[8,256]{1,0:T(8,128)S(1)}, f32[32,16,128]{2,1,0:T(8,128)S(1)}, ...), branch_computations={%region_0.1_spmd, %region_1.0_spmd} | conditional | flops 527616 | bytes 8400392 | solution.py:616
  5.7 73.4 %move_2.1 = (f32[256,16,128]{2,1,0:T(8,128)S(1)}, f32[256,16,128]{2,1,0:T(8,128)}, f32[2,1024,128]{2,1,0:T(8,128)S(1)}, f32[2,2,256,128]{3,2,1,0:T(8,128)}) custom-call(s32[8,256]{1,0:T(8,128)S(1)} %get-tuple-element.17.table_ref, f32[32,16,128]{2,1,0:T(8,128)S(1)} %get-tuple-element.18.send_ref, f32[1024,16,128]{2,1,0:T(8,128)} %get-tuple-element.19.a_ref), custom_call_target="tpu_custom_call" | custom-call | tf_op jit(solution)/shard_map/cond/branch_1_fun/move_2/pallas_call | solution.py:416
  79.1 0.0 copy-done
  79.1 17.6 %update.1 = f32[1024,16,128]{2,1,0:T(8,128)} custom-call(s32[8,256]{1,0:T(8,128)S(1)} %get-tuple-element.26.table_ref.place_ref, f32[2,128,128]{2,1,0:T(8,128)S(1)} %copy-done, s32[8,256]{1,0:T(8,128)S(1)} %get-tuple-element.26.table_ref.place_ref, f32[1024,16,128]{2,1,0:T(8,128)} %bitcast.12, f32[256,16,128]{2,1,0:T(8,128)S(1)} %get-tuple-element.28.new_ref, ...), custom_call_target="tpu_custom_call" | custom-call | tf_op jit(solution)/shard_map/update/pallas_call | solution.py:579
Async XLA Ops:
  5.6 73.4 %copy-start = (f32[2,128,128]{2,1,0:T(8,128)S(1)}, f32[2,128,128]{2,1,0:T(8,128)}, u32[]{:S(2)}) copy-start(f32[2,128,128]{2,1,0:T(8,128)} %inv_ref.1) | copy-start | bytes 393220

commit v2 on v1

v2 whole, which is shorter than its diff:
```python
import functools

import jax
import jax.numpy as jnp
from jax import lax
from jax.experimental import pallas as pl
from jax.experimental.pallas import tpu as pltpu
from jax.sharding import PartitionSpec as P

MESH = pl.DeviceIdType.MESH
NB = 128
NT = 256
DEV = 16
ROWS = 1024
FEW = 2
MANY = 16
OLD = {FEW: 2, MANY: 8}
MIB = 1 << 20

T_PLACE, T_FIX, T_COUNT, T_PICK, T_OUT, T_MID, T_MOST = range(7)


def iota(shape, dim):
    return lax.broadcasted_iota(jnp.int32, shape, dim)


def fiota(shape, dim):
    return iota(shape, dim).astype(jnp.float32)


def plan_kernel(k, piv_ref, a_ref, table_ref, send_ref, row_buf, row_smem, sem, row_sem):
    me = lax.axis_index("prow")
    old = OLD[k]
    sq = (NT, NT)
    sub, lane = fiota(sq, 0), fiota(sq, 1)
    diag = sub == lane
    lane1 = fiota((1, NT), 1)

    def to_col(row):
        row = row.astype(jnp.float32)
        return jnp.sum(jnp.where(diag, row, 0.0), axis=1, keepdims=True)

    def down(mask, value=1.0):
        return jnp.sum(jnp.where(mask, value, 0.0), axis=0, keepdims=True)

    def count(mask):
        return down(mask).astype(jnp.int32)

    def deal(cond, slot, value):
        slot_col = to_col(jnp.where(cond, slot, -1))
        return down(slot_col == lane, to_col(value)).astype(jnp.int32)

    def put(row, value):
        table_ref[row : row + 1, :] = jnp.broadcast_to(value, (1, NT)).astype(jnp.int32)

    piv = piv_ref[...].astype(jnp.float32)
    t_row = jnp.concatenate([piv[0:1, :], piv[1:2, :] + float(NB)], axis=1)
    t_col = to_col(t_row)
    before = sub < lane
    same = t_col == t_row
    last_same = jnp.max(jnp.where(same & before, sub, -1.0), axis=0, keepdims=True)
    later = jnp.max(jnp.where(same & (sub > lane), 1.0, 0.0), axis=0, keepdims=True)
    parent = jnp.max(jnp.where((t_col == lane) & before, sub, -1.0), axis=0, keepdims=True)
    c_row = jnp.where(parent < 0.0, lane1, parent)

    def jump(_, c_row):
        return down(sub == c_row, to_col(c_row))

    c_row = lax.fori_loop(0, 8, jump, c_row)

    from_swap = down(sub == last_same, to_col(c_row))
    src = jnp.where(last_same < 0.0, t_row, from_swap).astype(jnp.int32)
    owner = (src >> 7) & (DEV - 1)
    local = ((src >> 11) << 7) + (src & (NB - 1))
    owner_row, owner_col = owner.astype(jnp.float32), to_col(owner)
    less = owner_col < owner_row
    pos = count(less | ((owner_col == owner_row) & before))
    rank = pos - count(less)
    bin_, which = pos & (DEV - 1), rank >> 4
    send = deal((owner == me) & (which < k), bin_ * k + which, local)
    row_buf[0:1, :] = send
    to_smem = pltpu.make_async_copy(row_buf, row_smem, sem)
    to_smem.start()

    put(T_PLACE, bin_ * 16 + (pos >> 4))
    put(T_PICK, deal(bin_ == me, pos >> 4, owner * k + jnp.minimum(which, k - 1)))

    target, c = t_row.astype(jnp.int32), c_row.astype(jnp.int32)
    goes = (later < 0.5) & (target >= NT)
    to, block = (target >> 7) & (DEV - 1), c >> 7
    key = jnp.where(goes, block * DEV + to, 64)
    key_row, key_col = key.astype(jnp.float32), to_col(key)
    less = key_col < key_row
    pos = count(less | ((key_col == key_row) & before))
    rank_old = pos - count(less)
    pos = pos - count(key_col < (block * DEV).astype(jnp.float32))
    mid, slot, turn = pos & (DEV - 1), pos >> 4, rank_old >> 4
    fits = goes & (turn < old)
    put(T_OUT, deal(goes & (block == me), mid * 8 + slot, c & (NB - 1)))
    lane_of = block * old + turn
    put(T_MID, deal(fits & (mid == me), to * (2 * old) + lane_of, block * 8 + slot))
    mine = fits & (to == me)
    order = count(before & (to_col(jnp.where(mine, 1, 0)) > 0.5))
    dst = ((target >> 11) << 7) + (target & (NB - 1))
    put(T_FIX, deal(mine, order, dst * NT + mid * (2 * old) + lane_of))
    put(T_COUNT, jnp.sum(jnp.where(mine, 1.0, 0.0), axis=1, keepdims=True))
    most = jnp.maximum(rank, jnp.where(goes, rank_old, 0)).astype(jnp.float32)
    put(T_MOST, jnp.max(most, axis=1, keepdims=True))
    put(7, jnp.zeros((1, 1), jnp.int32))

    to_smem.wait()
    copies = [
        pltpu.make_async_copy(a_ref.at[row_smem[0, i]], send_ref.at[i], row_sem.at[i])
        for i in range(DEV * k)
    ]
    for copy in copies:
        copy.start()
    for copy in copies:
        copy.wait()


def plan(k, pivots, work):
    return pl.pallas_call(
        functools.partial(plan_kernel, k),
        out_shape=(
            jax.ShapeDtypeStruct((8, NT), jnp.int32),
            jax.ShapeDtypeStruct((DEV * k, DEV, NB), jnp.float32),
        ),
        in_specs=[pl.BlockSpec(memory_space=pltpu.VMEM), pl.BlockSpec(memory_space=pl.ANY)],
        out_specs=(pl.BlockSpec(memory_space=pltpu.VMEM), pl.BlockSpec(memory_space=pl.ANY)),
        scratch_shapes=[
            pltpu.VMEM((8, NT), jnp.int32),
            pltpu.SMEM((8, NT), jnp.int32),
            pltpu.SemaphoreType.DMA,
            pltpu.SemaphoreType.DMA((DEV * k,)),
        ],
        name=f"plan_{k}",
    )(pivots, work)


PIECES = 4


def move_kernel(
    k, table_ref, send_ref, a_ref,
    new_out, old_out, panel_out, top_out, side_out,
    got, mid, leave, leave2, first, new, old, panel, top, side,
    s_got, r_got, s_out, r_out, s_mid, r_mid, s_ag, r_ag, s_z, r_z, s_sib, r_sib,
    s_top, r_top, s_far, r_far, s_loc,
):
    me = lax.axis_index("prow")
    col = lax.axis_index("pcol")
    x, y = me // 4, me % 4
    z, core = col // 2, col % 2
    both = 2 * OLD[k]
    sends = []
    is_root, is_old = z == 0, me < 2

    def at(px, py):
        return (lax.rem(px + 4, 4) * 4 + lax.rem(py + 4, 4), col)

    def remote(src, dst, send_sem, recv_sem, device):
        return pltpu.make_async_remote_copy(
            src_ref=src, dst_ref=dst, send_sem=send_sem, recv_sem=recv_sem,
            device_id=device, device_id_type=MESH,
        )

    offsets = [(dx, dy) for dx in range(4) for dy in range(4) if (dx, dy) != (0, 0)]
    plane = [at(x + dx, y + dy) for dx, dy in offsets]
    origin = [at(x - dx, y - dy) for dx, dy in offsets]
    sibling = (me, z * 2 + 1 - core)
    others = [(me, lax.rem(z + i, 4) * 2 + core) for i in (1, 2, 3)]

    mine = pltpu.make_async_copy(a_ref.at[:, 0, :], panel.at[core], s_loc.at[0])
    block = pltpu.make_async_copy(a_ref.at[pl.ds(0, NB)], first, s_loc.at[1])

    @pl.when(is_root)
    def _():
        mine.start()

    @pl.when(is_old)
    def _():
        block.start()

    barrier = pltpu.get_barrier_semaphore()
    greeted = plane + others + [sibling]
    for device in greeted:
        pl.semaphore_signal(barrier, inc=1, device_id=device, device_id_type=MESH)

    @pl.when(is_old)
    def _():
        block.wait()

        @pl.loop(0, NB)
        def _(i):
            leave[i] = first[table_ref[T_OUT, i]]

    pl.semaphore_wait(barrier, len(greeted))

    def exchange(src, dst, n, s_sem, r_sem):
        for j, device in enumerate(plane):
            copy = remote(
                src.at[pl.ds(device[0] * n, n)], dst.at[pl.ds(me * n, n)],
                s_sem.at[j], r_sem.at[j], device,
            )
            copy.start()
            sends.append(copy)

    def exchanged(src, dst, n, s_sem, r_sem):
        for j, device in enumerate(origin):
            remote(
                src.at[pl.ds(0, n)], dst.at[pl.ds(device[0] * n, n)],
                s_sem.at[j], r_sem.at[j], device,
            ).wait_recv()

    exchange(send_ref, got, k, s_got, r_got)
    own = pltpu.make_async_copy(
        send_ref.at[pl.ds(me * k, k)], got.at[pl.ds(me * k, k)], s_loc.at[2]
    )
    own.start()

    stage = jnp.where(core == 0, z, lax.rem(4 - z, 4))
    onward = (me, jnp.where(core == 0, lax.rem(z + 1, 4), lax.rem(z + 3, 4)) * 2 + core)
    size = ROWS // PIECES

    def z_part(i):
        return panel.at[core, pl.ds(i * size, size)]

    def z_onward(i):
        return remote(z_part(i), z_part(i), s_z.at[i], r_z.at[i], onward)

    def z_sibling(i):
        return remote(z_part(i), z_part(i), s_sib.at[i], r_sib.at[i], sibling)

    def z_step(i):
        @pl.when(z > 0)
        def _():
            z_onward(i).wait_recv()

            @pl.when(stage < 3)
            def _():
                z_onward(i).start()

            z_sibling(i).start()

    def z_finish(i):
        @pl.when(stage < 3)
        def _():
            z_onward(i).wait_send()

        z_sibling(i).wait_send()
        part = panel.at[1 - core, pl.ds(i * size, size)]
        remote(part, part, s_sib.at[i], r_sib.at[i], sibling).wait_recv()

    @pl.when(is_root)
    def _():
        mine.wait()
        for i in range(PIECES):
            z_onward(i).start()
            z_sibling(i).start()

    def deal_out(half):
        return [
            remote(
                leave.at[pl.ds(device[0] * 8, 8)], mid.at[pl.ds(half * 8, 8)],
                s_out.at[j], r_out.at[half], device,
            )
            for j, device in enumerate(plane)
        ]

    def deal_own(half):
        return pltpu.make_async_copy(
            leave.at[pl.ds(me * 8, 8)], mid.at[pl.ds(half * 8, 8)], s_loc.at[3]
        )

    for half in range(2):

        @pl.when(me == half)
        def _():
            deal_own(half).start()
            for copy in deal_out(half):
                copy.start()

    def ring(axis, step):
        if axis == 0:
            return lax.rem(x + step + 4, 4) * 4 + y
        return x * 4 + lax.rem(y + step + 4, 4)

    def shifted(index, axis, step):
        px, py = index // 4, index % 4
        if axis == 0:
            return lax.rem(px + step + 4, 4) * 4 + py
        return px * 4 + lax.rem(py + step + 4, 4)

    def part_of(index, half, part=None):
        if part is None:
            return new.at[pl.ds(index * 16, 16), pl.ds(half * 8, 8)]
        return new.at[pl.ds(index * 16 + part * 8, 8), pl.ds(half * 8, 8)]

    class Gather:
        def __init__(self, half):
            self.half, self.base = half, half * 20
            self.axes = (0, 1) if half == 0 else (1, 0)

        def copy(self, phase, item, role, index, part=None):
            n = self.base + phase * (1 + item) * 4 + role
            ref = part_of(index, self.half, part)
            device = (ring(self.axes[phase], 1 if role % 2 == 0 else 3), col)
            return remote(ref, ref, s_ag.at[n], r_ag.at[n], device)

        def send(self, *args):
            copy = self.copy(*args)
            copy.start()
            sends.append(copy)

        def start(self, phase, item, index):
            for role in range(2):
                self.send(phase, item, role, index)

        def near(self, phase, item, index, role):
            came = shifted(index, self.axes[phase], 3 if role == 0 else 1)
            self.copy(phase, item, role, came).wait_recv()
            self.send(phase, item, 2 + role, came, role)
            return came

        def far(self, phase, item, index):
            came = shifted(index, self.axes[phase], 2)
            for role in range(2):
                self.copy(phase, item, 2 + role, came, role).wait_recv()
            return came

    exchanged(send_ref, got, k, s_got, r_got)
    own.wait()
    for i in range(16):
        new[me * 16 + i] = got[table_ref[T_PICK, i]]
    halves = [Gather(h) for h in range(2)]
    items = [[me], [me]]
    for g in halves:
        g.start(0, 0, me)
    for g in halves:
        g.start(1, 0, me)

    def top_part(index):
        return top.at[core, pl.ds(index * 16, 16)]

    def top_send(j):
        return remote(top_part(me), top_part(me), s_top.at[j], r_top.at[j], plane[j])

    def spread(kind, i):
        ref = (top if kind == 0 else side).at[core]
        return remote(ref, ref, s_far.at[kind, i], r_far.at[kind], others[i])

    def pass_on(kind):
        ref = (top if kind == 0 else side).at[core]
        n = PIECES + kind
        return remote(ref, ref, s_sib.at[n], r_sib.at[n], sibling)

    def from_sibling(kind):
        ref = (top if kind == 0 else side).at[1 - core]
        n = PIECES + kind
        return remote(ref, ref, s_sib.at[n], r_sib.at[n], sibling)

    @pl.when(is_root)
    def _():
        top[core, pl.ds(me * 16, 16), :] = new.reshape(NT * DEV, NB)[
            pl.ds(me * 16 * DEV, 16, stride=DEV), :
        ]
        for j in range(len(plane)):
            top_send(j).start()

    z_step(0)

    for half in range(2):

        @pl.when(me == half)
        def _():
            deal_own(half).wait()

        @pl.when(me != half)
        def _():
            ref = mid.at[pl.ds(half * 8, 8)]
            remote(ref, ref, s_out.at[0], r_out.at[half], plane[0]).wait_recv()

    for i in range(DEV * both):
        leave2[i] = mid[table_ref[T_MID, i]]
    exchange(leave2, old, both, s_mid, r_mid)
    own_old = pltpu.make_async_copy(
        leave2.at[pl.ds(me * both, both)], old.at[pl.ds(me * both, both)], s_loc.at[4]
    )
    own_old.start()

    z_step(1)
    for role in range(2):
        for h, g in enumerate(halves):
            came = g.near(0, 0, me, role)
            g.start(1, 1 + role, came)
            items[h].append(came)
    z_step(2)
    for h, g in enumerate(halves):
        came = g.far(0, 0, me)
        g.start(1, 3, came)
        items[h].append(came)
    z_step(3)

    @pl.when(is_root)
    def _():
        for j in range(len(plane)):
            index = origin[j][0]
            remote(
                top_part(index), top_part(index), s_top.at[j], r_top.at[j], plane[j]
            ).wait_recv()
        for i in range(3):
            spread(0, i).start()
        pass_on(0).start()

    def forward(i):
        for h, g in enumerate(halves):
            for role in range(2):
                g.near(1, i, items[h][i], role)

    forward(0)
    forward(1)

    @pl.when(z > 0)
    def _():
        spread(0, 0).wait_recv()
        pass_on(0).start()

    forward(2)
    forward(3)
    exchanged(leave2, old, both, s_mid, r_mid)
    own_old.wait()

    @pl.when(is_root)
    def _():
        side[core] = old.reshape(DEV * both * DEV, NB)[
            pl.ds(0, DEV * both, stride=DEV), :
        ]
        for i in range(3):
            spread(1, i).start()
        pass_on(1).start()

    def out(i, src, dst):
        return pltpu.make_async_copy(src, dst, s_loc.at[5 + i])

    outs = [out(0, old, old_out)]
    outs[0].start()
    for i in range(PIECES):
        z_finish(i)
    outs.append(out(1, panel, panel_out))
    outs[1].start()
    for i in range(4):
        for h, g in enumerate(halves):
            g.far(1, i, items[h][i])
    outs.append(out(2, new, new_out))
    outs[2].start()

    @pl.when(z > 0)
    def _():
        spread(1, 0).wait_recv()
        pass_on(1).start()

    for kind in range(2):
        from_sibling(kind).wait_recv()
    outs.append(out(3, top, top_out))
    outs.append(out(4, side, side_out))
    outs[3].start()
    outs[4].start()
    for kind in range(2):
        pass_on(kind).wait_send()

    @pl.when(is_root)
    def _():
        for kind in range(2):
            for i in range(3):
                spread(kind, i).wait_send()
        for j in range(len(plane)):
            top_send(j).wait_send()

    for half in range(2):

        @pl.when(me == half)
        def _():
            for copy in deal_out(half):
                copy.wait_send()

    for copy in sends:
        copy.wait_send()
    for copy in outs:
        copy.wait()


def move(k, table, send, work):
    both = 2 * OLD[k]
    outs = (
        (NT, DEV, NB),
        (DEV * both, DEV, NB),
        (2, ROWS, NB),
        (2, NT, NB),
        (2, DEV * both, NB),
    )
    dma = pltpu.SemaphoreType.DMA
    scratch = ((DEV * k, DEV, NB), (16, DEV, NB), (NB, DEV, NB), outs[1], (NB, DEV, NB)) + outs
    return pl.pallas_call(
        functools.partial(move_kernel, k),
        out_shape=tuple(jax.ShapeDtypeStruct(s, jnp.float32) for s in outs),
        in_specs=[
            pl.BlockSpec(memory_space=pltpu.SMEM),
            pl.BlockSpec(memory_space=pl.ANY),
            pl.BlockSpec(memory_space=pl.ANY),
        ],
        out_specs=tuple(pl.BlockSpec(memory_space=pl.ANY) for _ in outs),
        scratch_shapes=[pltpu.VMEM(s, jnp.float32) for s in scratch]
        + [
            dma((15,)), dma((15,)), dma((15,)), dma((2,)), dma((15,)), dma((15,)),
            dma((40,)), dma((40,)), dma((PIECES,)), dma((PIECES,)),
            dma((PIECES + 2,)), dma((PIECES + 2,)), dma((15,)), dma((15,)),
            dma((2, 3)), dma((2,)), dma((10,)),
        ],
        compiler_params=pltpu.CompilerParams(
            collective_id=k, has_side_effects=True, vmem_limit_bytes=24 * MIB
        ),
        name=f"move_{k}",
    )(table, send, work)


def split(a):
    hi = a.astype(jnp.bfloat16)
    return hi, (a - hi.astype(jnp.float32)).astype(jnp.bfloat16)


def dot(a, b):
    return jnp.dot(a, b, preferred_element_type=jnp.float32)


def dot3(a, b):
    return dot(a[0], b[0]) + (dot(a[0], b[1]) + dot(a[1], b[0]))


CHUNKS = 4
CROWS = ROWS // CHUNKS


def update_kernel(
    n_old, table_ref, inv_ref, place_ref, a_ref, new_ref, old_ref, panel_ref, top_ref, side_ref,
    out_ref,
    a, rows, panel, top, b_hi, b_lo, g_hi, g_lo, sems,
):
    me = lax.axis_index("prow")
    col = lax.axis_index("pcol")
    loads = [
        pltpu.make_async_copy(panel_ref, panel, sems.at[0]),
        pltpu.make_async_copy(top_ref, top.at[:, pl.ds(0, NT)], sems.at[1]),
        pltpu.make_async_copy(side_ref, top.at[:, pl.ds(NT, n_old)], sems.at[2]),
        pltpu.make_async_copy(new_ref, rows.at[pl.ds(0, NT)], sems.at[3]),
        pltpu.make_async_copy(old_ref, rows.at[pl.ds(NT, n_old)], sems.at[4]),
    ]
    a_loads = [
        pltpu.make_async_copy(
            a_ref.at[pl.ds(i * CROWS, CROWS)], a.at[pl.ds(i * CROWS, CROWS)], sems.at[5 + i]
        )
        for i in range(CHUNKS)
    ]
    for copy in loads + a_loads:
        copy.start()
    for copy in loads[:3]:
        copy.wait()

    count = table_ref[T_COUNT, 0]

    def fix_panel(dst, src):
        for p in range(2):
            panel[p, pl.ds(dst, 1), :] = top[p, pl.ds(src, 1), :]

    def fix_row(dst, src):
        a[dst] = rows[src]

    def fix_all(fix):
        @pl.when(me < 2)
        def _():
            @pl.loop(0, NB)
            def _(i):
                fix(i, table_ref[T_PLACE, me * NB + i])

        @pl.loop(0, count)
        def _(i):
            entry = table_ref[T_FIX, i]
            fix(entry >> 8, NT + (entry & (NT - 1)))

    fix_all(fix_panel)

    place = place_ref[T_PLACE : T_PLACE + 1, :]
    order_t = jnp.where(iota((NT, NT), 0) == place, 1.0, 0.0).astype(jnp.bfloat16)

    def pick(lo, val):
        return lax.dot_general(
            order_t[:, lo : lo + NB], val, (((0,), (0,)), ((), ())),
            preferred_element_type=jnp.float32,
        )

    inv = [split(inv_ref[s]) for s in range(2)]
    u_split = split(top[1, 0:NT, :])
    u0p = tuple(pick(0, v).astype(jnp.bfloat16) for v in u_split)
    p_split = split(top[0, 0:NT, :])
    l0b = dot3(tuple(pick(NB, v).astype(jnp.bfloat16) for v in p_split), inv[0])
    l0b = split(l0b)

    for i in range(CHUNKS):
        part = pl.ds(i * CROWS, CROWS)
        l0 = dot3(split(panel[0, part, :]), inv[0])
        if i == 0:
            top_rows = iota((CROWS, NB), 0) < NB
            l0 = jnp.where(top_rows & (me == 0), 0.0, l0)
        rest = panel[1, part, :] - dot3(split(l0), u0p)
        l1 = dot3(split(rest), inv[1])
        if i == 0:
            l1 = jnp.where(top_rows & (me < 2), 0.0, l1)
        g0 = l0 - dot3(split(l1), l0b)
        panel[0, part, :] = l0
        panel[1, part, :] = l1
        g = split(jnp.concatenate([g0, l1], axis=1))
        for ref, val in ((g_hi, g[0]), (g_lo, g[1])):
            ref[part, :] = lax.dot_general(
                val, order_t, (((1,), (1,)), ((), ())), preferred_element_type=jnp.float32
            ).astype(jnp.bfloat16)

    for copy in loads[3:]:
        copy.wait()
    flat = rows.reshape((NT + n_old) * DEV, NB)
    for c in range(DEV):
        hi, lo = split(flat[pl.ds(c, NT, stride=DEV), :])
        b_hi[:, c * NB : (c + 1) * NB] = hi
        b_lo[:, c * NB : (c + 1) * NB] = lo
    for copy in a_loads:
        copy.wait()
    fix_all(fix_row)

    aflat = a.reshape(ROWS * DEV, NB)
    stores = []
    for i in range(CHUNKS):
        part = pl.ds(i * CROWS, CROWS)

        for c in range(0, DEV, 2):
            wide = slice(c * NB, (c + 2) * NB)
            upd = dot3((g_hi[part, :], g_lo[part, :]), (b_hi[:, wide], b_lo[:, wide]))
            for h in range(2):
                where = pl.ds(i * CROWS * DEV + c + h, CROWS, stride=DEV)
                base = aflat[where, :]
                val = base - upd[:, h * NB : (h + 1) * NB]
                if c + h == 0:
                    fac = jnp.where(col == 0, panel[0, part, :], panel[1, part, :])
                    if i == 0:
                        top_rows = iota((CROWS, NB), 0) < NB
                        keep = jnp.where(col == 0, me == 0, me < 2)
                        same = top_rows & keep
                        base_or = jnp.where(col == 0, base, val)
                        fac = jnp.where(same, base_or, fac)
                    val = jnp.where(col < 2, fac, val)
                aflat[where, :] = val
        store = pltpu.make_async_copy(a.at[part], out_ref.at[part], sems.at[5 + i])
        store.start()
        stores.append(store)
    for store in stores:
        store.wait()


def update(table, inverses, work, new, old, panel, top, side):
    n_old = old.shape[0]
    any_ = pl.BlockSpec(memory_space=pl.ANY)
    return pl.pallas_call(
        functools.partial(update_kernel, n_old),
        out_shape=jax.ShapeDtypeStruct((ROWS, DEV, NB), jnp.float32),
        in_specs=[
            pl.BlockSpec(memory_space=pltpu.SMEM),
            pl.BlockSpec(memory_space=pltpu.VMEM),
            pl.BlockSpec(memory_space=pltpu.VMEM),
            any_, any_, any_, any_, any_, any_,
        ],
        out_specs=any_,
        scratch_shapes=[
            pltpu.VMEM((ROWS, DEV, NB), jnp.float32),
            pltpu.VMEM((NT + n_old, DEV, NB), jnp.float32),
            pltpu.VMEM((2, ROWS, NB), jnp.float32),
            pltpu.VMEM((2, NT + n_old, NB), jnp.float32),
            pltpu.VMEM((NT, DEV * NB), jnp.bfloat16),
            pltpu.VMEM((NT, DEV * NB), jnp.bfloat16),
            pltpu.VMEM((ROWS, NT), jnp.bfloat16),
            pltpu.VMEM((ROWS, NT), jnp.bfloat16),
            pltpu.SemaphoreType.DMA((5 + CHUNKS,)),
        ],
        compiler_params=pltpu.CompilerParams(vmem_limit_bytes=40 * MIB),
        name=f"update_{n_old}",
    )(table, inverses, table, work, new, old, panel, top, side)


def on_device(matrix, pivots, block_inverses):
    work = matrix.reshape(ROWS, DEV, NB)
    table, send = plan(FEW, pivots, work)

    def few():
        return update(table, block_inverses, work, *move(FEW, table, send, work))

    def many():
        table, send = plan(MANY, pivots, work)
        return update(table, block_inverses, work, *move(MANY, table, send, work))

    out = lax.cond(table[T_MOST, 0] < FEW * DEV, few, many)
    return out.reshape(matrix.shape)


def solution(mesh):
    in_specs = (P(None, "prow", None, None, "pcol", None), P(), P())
    out_specs = P(None, "prow", None, None, "pcol", None)
    return jax.shard_map(
        on_device, mesh=mesh, in_specs=in_specs, out_specs=out_specs, check_vma=False
    )
```

time: 97.1 us -> 72.9 us (0.75)
  Pallas kernels: 95.5 us -> 67.8 us
  local copies, waits for them, and re-layouts: 0.52 us -> 3.92 us
    pallas_call x1, Pallas kernels: 73.4 us -> 47 us  [move(): pl.pallas_call(functools.partial(move_kernel, k), out_shape=tuple((jax.Sh...]
    unnamed x2 -> x6, local copies, waits for them, and re-layouts: 0.01 us -> 3.4 us
    pallas_call x2, Pallas kernels: 22.1 us -> 20.9 us  [the longest x1 16.2 us: update(): pl.pallas_call(functools.partial(update_kernel, n_old), out_shape=jax.Sha...]
where the time goes in v2:
time: 72.9 us; the launch traced here: 72.7 us
  Pallas kernels  67.8 us (93%)
  local copies, waits for them, and re-layouts  3.92 us (5%)
    pallas_call x1, Pallas kernels, move(): pl.pallas_call(functools.partial(move_kernel, k), out_shape=tuple((jax.Sh...  47 us
    pallas_call x1, Pallas kernels, update(): pl.pallas_call(functools.partial(update_kernel, n_old), out_shape=jax.Sha...  16.2 us
    pallas_call x1, Pallas kernels, plan(): pl.pallas_call(functools.partial(plan_kernel, k), out_shape=(jax.ShapeDty...  4.7 us
    unnamed x6, local copies, waits for them, and re-layouts  3.4 us

profile of v2, /device:TPU:97, one launch (start us, length us, event | category | flops | bytes accessed | tf_op | source)
XLA Modules:
  0.0 72.7 jit_solution(3083993372035227020)
XLA Ops:
  0.0 0.0 copy-start.5
  0.0 0.0 copy-start.6
  0.0 4.7 %plan_2.1 = (s32[8,256]{1,0:T(8,128)S(1)}, f32[32,16,128]{2,1,0:T(8,128)S(1)}) custom-call(s32[2,128]{1,0:T(2,128)} %piv_ref.1, f32[1024,16,128]{2,1,0:T(8,128)} %bitcast.8), custom_call_target="tpu_custom_call" | custom-call | tf_op jit(solution)/shard_map/plan_2/pallas_call | solution.py:123
  4.7 0.5 slice.3
  5.9 0.0 copy-done.5
  5.9 0.0 copy-done.6
  5.9 63.4 %conditional.1 = (f32[8,1,128,16,1,128]{5,4,3,2,1,0:T(1,128)S(1)}) conditional(s32[]{:T(128)} %bitcast.7, (s32[2,128]{1,0:T(2,128)S(1)}, f32[1024,16,128]{2,1,0:T(8,128)}, f32[2,128,128]{2,1,0:T(8,128)S(1)}) %tuple.26, (s32[8,256]{1,0:T(8,128)S(1)}, f32[32,16,128]{2,1,0:T(8,128)S(1)}, f32[1024,16,128]{2,1,0:T(8,128)}, ...), branch_computations={%region_0.0_spmd, %region_1.0_spmd} | conditional | bytes 33554468 | solution.py:707
  6.1 0.0 copy-start.3
  6.2 47.0 %move_2.1 = (f32[256,16,128]{2,1,0:T(8,128)S(1)}, f32[64,16,128]{2,1,0:T(8,128)S(1)}, f32[2,1024,128]{2,1,0:T(8,128)S(1)}, f32[2,256,128]{2,1,0:T(8,128)S(1)}, f32[2,64,128]{2,1,0:T(8,128)S(1)}) custom-call(s32[8,256]{1,0:T(8,128)S(1)} %get-tuple-element.33.table_ref.place_ref, f32[32,16,128]{2,1,0:T(8,128)S(1)} %get-tuple-element.36.send_ref, ...), custom_call_target="tpu_custom_call" | custom-call | tf_op jit(solution)/shard_map/cond/branch_1_fun/move_2/pallas_call | solution.py:504
  53.1 0.0 copy-done.3
  53.2 16.2 %update_64.1 = f32[1024,16,128]{2,1,0:T(8,128)S(1)} custom-call(s32[8,256]{1,0:T(8,128)S(1)} %get-tuple-element.33.table_ref.place_ref, f32[2,128,128]{2,1,0:T(8,128)S(1)} %get-tuple-element.34.inv_ref, s32[8,256]{1,0:T(8,128)S(1)} %get-tuple-element.33.table_ref.place_ref, f32[1024,16,128]{2,1,0:T(8,128)S(1)} %copy-done.3, ...), custom_call_target="tpu_custom_call" | custom-call | tf_op jit(solution)/shard_map/cond/branch_1_fun/update_64/pallas_call | solution.py:670
  69.3 0.0 copy-start.4
  69.3 3.4 %copy-done.4 = f32[8,1,128,16,1,128]{5,4,3,2,1,0:T(1,128)} copy-done((f32[8,1,128,16,1,128]{5,4,3,2,1,0:T(1,128)}, f32[8,1,128,16,1,128]{5,4,3,2,1,0:T(1,128)S(1)}, u32[]{:S(2)}) %copy-start.4) | copy-done | bytes 8388632
Async XLA Ops:
  0.0 5.9 %copy-start.5 = (f32[2,128,128]{2,1,0:T(8,128)S(1)}, f32[2,128,128]{2,1,0:T(8,128)}, u32[]{:S(2)}) copy-start(f32[2,128,128]{2,1,0:T(8,128)} %param.7) | copy-start | bytes 393220
  0.0 5.9 %copy-start.6 = (s32[2,128]{1,0:T(2,128)S(1)}, s32[2,128]{1,0:T(2,128)}, u32[]{:S(2)}) copy-start(s32[2,128]{1,0:T(2,128)} %piv_ref.1) | copy-start | bytes 3076
  6.1 47.0 %copy-start.3 = (f32[1024,16,128]{2,1,0:T(8,128)S(1)}, f32[1024,16,128]{2,1,0:T(8,128)}, u32[]{:S(2)}) copy-start(f32[1024,16,128]{2,1,0:T(8,128)} %get-tuple-element.35.a_ref) | copy-start | bytes 25165828 | tf_op jit(solution)/shard_map/cond
  69.3 3.4 %copy-start.4 = (f32[8,1,128,16,1,128]{5,4,3,2,1,0:T(1,128)}, f32[8,1,128,16,1,128]{5,4,3,2,1,0:T(1,128)S(1)}, u32[]{:S(2)}) copy-start(f32[8,1,128,16,1,128]{5,4,3,2,1,0:T(1,128)S(1)} %get-tuple-element.50) | copy-start | bytes 25165828

commit v3 on v2

--- a/solution.py
+++ b/solution.py
@@ -14,10 +14,11 @@
 ROWS = 1024
 FEW = 2
 MANY = 16
-OLD = {FEW: 2, MANY: 8}
+OLD = {FEW: 3, MANY: 16}
+N_OLD = {k: DEV * n for k, n in OLD.items()}
 MIB = 1 << 20
 
-T_PLACE, T_FIX, T_COUNT, T_PICK, T_OUT, T_MID, T_MOST = range(7)
+T_PLACE, T_FIX, T_COUNT, T_PICK, T_OUT, T_MID, T_OVER = range(7)
 
 
 def iota(shape, dim):
@@ -92,20 +93,19 @@
     key_row, key_col = key.astype(jnp.float32), to_col(key)
     less = key_col < key_row
     pos = count(less | ((key_col == key_row) & before))
-    rank_old = pos - count(less)
     pos = pos - count(key_col < (block * DEV).astype(jnp.float32))
-    mid, slot, turn = pos & (DEV - 1), pos >> 4, rank_old >> 4
-    fits = goes & (turn < old)
+    mid, slot = pos & (DEV - 1), pos >> 4
+    pair = jnp.where(goes, to * DEV + mid, NT)
+    turn = count((to_col(pair) == pair.astype(jnp.float32)) & before)
     put(T_OUT, deal(goes & (block == me), mid * 8 + slot, c & (NB - 1)))
-    lane_of = block * old + turn
-    put(T_MID, deal(fits & (mid == me), to * (2 * old) + lane_of, block * 8 + slot))
-    mine = fits & (to == me)
+    put(T_MID, deal(goes & (turn < old) & (mid == me), to * old + turn, block * 8 + slot))
+    mine = goes & (to == me)
     order = count(before & (to_col(jnp.where(mine, 1, 0)) > 0.5))
     dst = ((target >> 11) << 7) + (target & (NB - 1))
-    put(T_FIX, deal(mine, order, dst * NT + mid * (2 * old) + lane_of))
+    put(T_FIX, deal(mine, order, dst * NT + mid * DEV + turn))
     put(T_COUNT, jnp.sum(jnp.where(mine, 1.0, 0.0), axis=1, keepdims=True))
-    most = jnp.maximum(rank, jnp.where(goes, rank_old, 0)).astype(jnp.float32)
-    put(T_MOST, jnp.max(most, axis=1, keepdims=True))
+    over = (which >= k) | (goes & (turn >= old))
+    put(T_OVER, jnp.max(jnp.where(over, 1.0, 0.0), axis=1, keepdims=True))
     put(7, jnp.zeros((1, 1), jnp.int32))
 
     to_smem.wait()
@@ -138,13 +138,26 @@
     )(pivots, work)
 
 
+def split(a):
+    hi = a.astype(jnp.bfloat16)
+    return hi, (a - hi.astype(jnp.float32)).astype(jnp.bfloat16)
+
+
+def dot(a, b):
+    return jnp.dot(a, b, preferred_element_type=jnp.float32)
+
+
+def dot3(a, b):
+    return dot(a[0], b[0]) + (dot(a[0], b[1]) + dot(a[1], b[0]))
+
+
 PIECES = 4
 
 
 def move_kernel(
-    k, table_ref, send_ref, a_ref,
-    new_out, old_out, panel_out, top_out, side_out,
-    got, mid, leave, leave2, first, new, old, panel, top, side,
+    k, table_ref, place_ref, inv_ref, send_ref, a_ref,
+    new, old, g_ref, fac_ref, side_g,
+    got, mid, leave, leave2, first, panel, top, side,
     s_got, r_got, s_out, r_out, s_mid, r_mid, s_ag, r_ag, s_z, r_z, s_sib, r_sib,
     s_top, r_top, s_far, r_far, s_loc,
 ):
@@ -152,7 +165,7 @@
     col = lax.axis_index("pcol")
     x, y = me // 4, me % 4
     z, core = col // 2, col % 2
-    both = 2 * OLD[k]
+    both = OLD[k]
     sends = []
     is_root, is_old = z == 0, me < 2
 
@@ -369,6 +382,16 @@
             top_send(j).start()
 
     z_step(0)
+    for role in range(2):
+        for h, g in enumerate(halves):
+            came = g.near(0, 0, me, role)
+            g.start(1, 1 + role, came)
+            items[h].append(came)
+    z_step(1)
+    for h, g in enumerate(halves):
+        came = g.far(0, 0, me)
+        g.start(1, 3, came)
+        items[h].append(came)
 
     for half in range(2):
 
@@ -389,17 +412,7 @@
     )
     own_old.start()
 
-    z_step(1)
-    for role in range(2):
-        for h, g in enumerate(halves):
-            came = g.near(0, 0, me, role)
-            g.start(1, 1 + role, came)
-            items[h].append(came)
     z_step(2)
-    for h, g in enumerate(halves):
-        came = g.far(0, 0, me)
-        g.start(1, 3, came)
-        items[h].append(came)
     z_step(3)
 
     @pl.when(is_root)
@@ -433,39 +446,66 @@
 
     @pl.when(is_root)
     def _():
-        side[core] = old.reshape(DEV * both * DEV, NB)[
-            pl.ds(0, DEV * both, stride=DEV), :
-        ]
+        side[core] = old.reshape(N_OLD[MANY] * DEV, NB)[pl.ds(0, DEV * both, stride=DEV), :]
         for i in range(3):
             spread(1, i).start()
         pass_on(1).start()
 
-    def out(i, src, dst):
-        return pltpu.make_async_copy(src, dst, s_loc.at[5 + i])
-
-    outs = [out(0, old, old_out)]
-    outs[0].start()
     for i in range(PIECES):
         z_finish(i)
-    outs.append(out(1, panel, panel_out))
-    outs[1].start()
+    from_sibling(0).wait_recv()
+
+    place = place_ref[T_PLACE : T_PLACE + 1, :]
+    order_t = jnp.where(iota((NT, NT), 0) == place, 1.0, 0.0).astype(jnp.bfloat16)
+
+    def pick(lo, val):
+        return lax.dot_general(
+            order_t[:, lo : lo + NB], val, (((0,), (0,)), ((), ())),
+            preferred_element_type=jnp.float32,
+        ).astype(jnp.bfloat16)
+
+    inv = [split(inv_ref[s]) for s in range(2)]
+    u0p = tuple(pick(0, v) for v in split(top[1]))
+    l0b_full = dot3(tuple(pick(NB, v) for v in split(top[0])), inv[0])
+    l0b = split(l0b_full)
+
+    def factors(p0, p1):
+        l0 = dot3(split(p0), inv[0])
+        l1 = dot3(split(p1 - dot3(split(l0), u0p)), inv[1])
+        return l0, l0 - dot3(split(l1), l0b), l1
+
+    for i in range(4):
+        part = pl.ds(i * 256, 256)
+        l0, g0, l1 = factors(panel[0, part, :], panel[1, part, :])
+        fac_ref[part, :] = l0
+        g_ref[part, 0:NB] = g0
+        g_ref[part, NB:] = l1
+
+    unit = jnp.where(iota((NB, NB), 0) == iota((NB, NB), 1), -1.0, 0.0)
+
+    @pl.when(me == 0)
+    def _():
+        g_ref[0:NB, 0:NB] = unit
+        g_ref[0:NB, NB:] = jnp.zeros((NB, NB), jnp.float32)
+
+    @pl.when(me == 1)
+    def _():
+        g_ref[0:NB, 0:NB] = l0b_full
+        g_ref[0:NB, NB:] = unit
+        fac_ref[0:NB, :] = l0b_full
+
+    @pl.when(z > 0)
+    def _():
+        spread(1, 0).wait_recv()
+        pass_on(1).start()
+
+    from_sibling(1).wait_recv()
+    for j, val in enumerate(factors(side[0], side[1])):
+        side_g[0 : DEV * both, j * NB : (j + 1) * NB] = val
     for i in range(4):
         for h, g in enumerate(halves):
             g.far(1, i, items[h][i])
-    outs.append(out(2, new, new_out))
-    outs[2].start()
-
-    @pl.when(z > 0)
-    def _():
-        spread(1, 0).wait_recv()
-        pass_on(1).start()
-
-    for kind in range(2):
-        from_sibling(kind).wait_recv()
-    outs.append(out(3, top, top_out))
-    outs.append(out(4, side, side_out))
-    outs[3].start()
-    outs[4].start()
+
     for kind in range(2):
         pass_on(kind).wait_send()
 
@@ -486,211 +526,149 @@
 
     for copy in sends:
         copy.wait_send()
-    for copy in outs:
-        copy.wait()
-
-
-def move(k, table, send, work):
-    both = 2 * OLD[k]
-    outs = (
-        (NT, DEV, NB),
-        (DEV * both, DEV, NB),
-        (2, ROWS, NB),
-        (2, NT, NB),
-        (2, DEV * both, NB),
+
+
+def move(k, table, inverses, send, work):
+    both = OLD[k]
+    dma = pltpu.SemaphoreType.DMA
+    outs = ((NT, DEV, NB), (N_OLD[MANY], DEV, NB), (ROWS, 2 * NB), (ROWS, NB), (N_OLD[MANY], 3 * NB))
+    scratch = (
+        (DEV * k, DEV, NB), (16, DEV, NB), (NB, DEV, NB), (DEV * both, DEV, NB), (NB, DEV, NB),
+        (2, ROWS, NB), (2, NT, NB), (2, DEV * both, NB),
     )
-    dma = pltpu.SemaphoreType.DMA
-    scratch = ((DEV * k, DEV, NB), (16, DEV, NB), (NB, DEV, NB), outs[1], (NB, DEV, NB)) + outs
+    any_ = pl.BlockSpec(memory_space=pl.ANY)
+    vmem = pl.BlockSpec(memory_space=pltpu.VMEM)
     return pl.pallas_call(
         functools.partial(move_kernel, k),
         out_shape=tuple(jax.ShapeDtypeStruct(s, jnp.float32) for s in outs),
-        in_specs=[
-            pl.BlockSpec(memory_space=pltpu.SMEM),
-            pl.BlockSpec(memory_space=pl.ANY),
-            pl.BlockSpec(memory_space=pl.ANY),
-        ],
-        out_specs=tuple(pl.BlockSpec(memory_space=pl.ANY) for _ in outs),
+        in_specs=[pl.BlockSpec(memory_space=pltpu.SMEM), vmem, vmem, any_, any_],
+        out_specs=(vmem,) * len(outs),
         scratch_shapes=[pltpu.VMEM(s, jnp.float32) for s in scratch]
         + [
             dma((15,)), dma((15,)), dma((15,)), dma((2,)), dma((15,)), dma((15,)),
             dma((40,)), dma((40,)), dma((PIECES,)), dma((PIECES,)),
             dma((PIECES + 2,)), dma((PIECES + 2,)), dma((15,)), dma((15,)),
-            dma((2, 3)), dma((2,)), dma((10,)),
+            dma((2, 3)), dma((2,)), dma((5,)),
         ],
         compiler_params=pltpu.CompilerParams(
-            collective_id=k, has_side_effects=True, vmem_limit_bytes=24 * MIB
+            collective_id=k, has_side_effects=True, vmem_limit_bytes=32 * MIB
         ),
         name=f"move_{k}",
-    )(table, send, work)
-
-
-def split(a):
-    hi = a.astype(jnp.bfloat16)
-    return hi, (a - hi.astype(jnp.float32)).astype(jnp.bfloat16)
-
-
-def dot(a, b):
-    return jnp.dot(a, b, preferred_element_type=jnp.float32)
-
-
-def dot3(a, b):
-    return dot(a[0], b[0]) + (dot(a[0], b[1]) + dot(a[1], b[0]))
+    )(table, table, inverses, send, work)
 
 
 CHUNKS = 4
 CROWS = ROWS // CHUNKS
+PITCH = 24
 
 
 def update_kernel(
-    n_old, table_ref, inv_ref, place_ref, a_ref, new_ref, old_ref, panel_ref, top_ref, side_ref,
+    table_ref, place_ref, a_ref, new_ref, old_ref, g_ref, fac_ref, side_ref,
     out_ref,
-    a, rows, panel, top, b_hi, b_lo, g_hi, g_lo, sems,
+    a, b3, g3, g, fac, sems,
 ):
     me = lax.axis_index("prow")
     col = lax.axis_index("pcol")
+    few = table_ref[T_OVER, 0] == 0
+    parts = [pl.ds(i * CROWS, CROWS) for i in range(CHUNKS)]
     loads = [
-        pltpu.make_async_copy(panel_ref, panel, sems.at[0]),
-        pltpu.make_async_copy(top_ref, top.at[:, pl.ds(0, NT)], sems.at[1]),
-        pltpu.make_async_copy(side_ref, top.at[:, pl.ds(NT, n_old)], sems.at[2]),
-        pltpu.make_async_copy(new_ref, rows.at[pl.ds(0, NT)], sems.at[3]),
-        pltpu.make_async_copy(old_ref, rows.at[pl.ds(NT, n_old)], sems.at[4]),
+        pltpu.make_async_copy(a_ref.at[part], a.at[part, pl.ds(0, DEV)], sems.at[i])
+        for i, part in enumerate(parts)
     ]
-    a_loads = [
-        pltpu.make_async_copy(
-            a_ref.at[pl.ds(i * CROWS, CROWS)], a.at[pl.ds(i * CROWS, CROWS)], sems.at[5 + i]
-        )
-        for i in range(CHUNKS)
-    ]
-    for copy in loads + a_loads:
+    for copy in loads:
         copy.start()
-    for copy in loads[:3]:
-        copy.wait()
-
-    count = table_ref[T_COUNT, 0]
-
-    def fix_panel(dst, src):
-        for p in range(2):
-            panel[p, pl.ds(dst, 1), :] = top[p, pl.ds(src, 1), :]
-
-    def fix_row(dst, src):
-        a[dst] = rows[src]
-
-    def fix_all(fix):
-        @pl.when(me < 2)
-        def _():
-            @pl.loop(0, NB)
-            def _(i):
-                fix(i, table_ref[T_PLACE, me * NB + i])
-
-        @pl.loop(0, count)
+
+    def each_fix(fix):
+        @pl.loop(0, table_ref[T_COUNT, 0])
         def _(i):
             entry = table_ref[T_FIX, i]
-            fix(entry >> 8, NT + (entry & (NT - 1)))
-
-    fix_all(fix_panel)
+            src = entry & (NT - 1)
+            packed = (src >> 4) * OLD[FEW] + (src & (DEV - 1))
+            fix(entry >> 8, jnp.where(few, packed, src))
+
+    g[...] = g_ref[...]
+    fac[...] = fac_ref[...]
+
+    def fix_factors(dst, src):
+        row = side_ref[pl.ds(src, 1), :]
+        g[pl.ds(dst, 1), :] = row[:, NB:]
+        fac[pl.ds(dst, 1), :] = row[:, 0:NB]
+
+    each_fix(fix_factors)
 
     place = place_ref[T_PLACE : T_PLACE + 1, :]
     order_t = jnp.where(iota((NT, NT), 0) == place, 1.0, 0.0).astype(jnp.bfloat16)
-
-    def pick(lo, val):
-        return lax.dot_general(
-            order_t[:, lo : lo + NB], val, (((0,), (0,)), ((), ())),
-            preferred_element_type=jnp.float32,
-        )
-
-    inv = [split(inv_ref[s]) for s in range(2)]
-    u_split = split(top[1, 0:NT, :])
-    u0p = tuple(pick(0, v).astype(jnp.bfloat16) for v in u_split)
-    p_split = split(top[0, 0:NT, :])
-    l0b = dot3(tuple(pick(NB, v).astype(jnp.bfloat16) for v in p_split), inv[0])
-    l0b = split(l0b)
-
-    for i in range(CHUNKS):
-        part = pl.ds(i * CROWS, CROWS)
-        l0 = dot3(split(panel[0, part, :]), inv[0])
-        if i == 0:
-            top_rows = iota((CROWS, NB), 0) < NB
-            l0 = jnp.where(top_rows & (me == 0), 0.0, l0)
-        rest = panel[1, part, :] - dot3(split(l0), u0p)
-        l1 = dot3(split(rest), inv[1])
-        if i == 0:
-            l1 = jnp.where(top_rows & (me < 2), 0.0, l1)
-        g0 = l0 - dot3(split(l1), l0b)
-        panel[0, part, :] = l0
-        panel[1, part, :] = l1
-        g = split(jnp.concatenate([g0, l1], axis=1))
-        for ref, val in ((g_hi, g[0]), (g_lo, g[1])):
-            ref[part, :] = lax.dot_general(
+    flat = new_ref.reshape(NT * DEV, NB)
+    for c in range(DEV):
+        hi, lo = split(flat[pl.ds(c, NT, stride=DEV), :])
+        for j, val in enumerate((hi, lo, hi)):
+            b3[j * NT : (j + 1) * NT, c * NB : (c + 1) * NB] = val
+    for part in parts:
+        g_hi, g_lo = (
+            lax.dot_general(
                 val, order_t, (((1,), (1,)), ((), ())), preferred_element_type=jnp.float32
             ).astype(jnp.bfloat16)
-
-    for copy in loads[3:]:
-        copy.wait()
-    flat = rows.reshape((NT + n_old) * DEV, NB)
-    for c in range(DEV):
-        hi, lo = split(flat[pl.ds(c, NT, stride=DEV), :])
-        b_hi[:, c * NB : (c + 1) * NB] = hi
-        b_lo[:, c * NB : (c + 1) * NB] = lo
-    for copy in a_loads:
-        copy.wait()
-    fix_all(fix_row)
-
-    aflat = a.reshape(ROWS * DEV, NB)
+            for val in split(g[part, :])
+        )
+        for j, val in enumerate((g_hi, g_hi, g_lo)):
+            g3[part, j * NT : (j + 1) * NT] = val
+
+    aflat = a.reshape(ROWS * PITCH, NB)
     stores = []
-    for i in range(CHUNKS):
-        part = pl.ds(i * CROWS, CROWS)
+    for i, part in enumerate(parts):
+        loads[i].wait()
+
+        def fix_row(dst, src):
+            @pl.when((dst >> 8) == i)
+            def _():
+                a[dst, 0:DEV, :] = old_ref[src]
+
+        each_fix(fix_row)
+        if i == 0:
+            @pl.when(me < 2)
+            def _():
+                a[0:NB, 0:DEV, :] = jnp.zeros((NB, DEV, NB), jnp.float32)
 
         for c in range(0, DEV, 2):
-            wide = slice(c * NB, (c + 2) * NB)
-            upd = dot3((g_hi[part, :], g_lo[part, :]), (b_hi[:, wide], b_lo[:, wide]))
+            upd = dot(g3[part, :], b3[:, c * NB : (c + 2) * NB])
             for h in range(2):
-                where = pl.ds(i * CROWS * DEV + c + h, CROWS, stride=DEV)
-                base = aflat[where, :]
-                val = base - upd[:, h * NB : (h + 1) * NB]
+                where = pl.ds(i * CROWS * PITCH + c + h, CROWS, stride=PITCH)
+                val = aflat[where, :] - upd[:, h * NB : (h + 1) * NB]
                 if c + h == 0:
-                    fac = jnp.where(col == 0, panel[0, part, :], panel[1, part, :])
+                    own = jnp.where(col == 0, fac[part, :], g[part, NB:])
                     if i == 0:
-                        top_rows = iota((CROWS, NB), 0) < NB
                         keep = jnp.where(col == 0, me == 0, me < 2)
-                        same = top_rows & keep
-                        base_or = jnp.where(col == 0, base, val)
-                        fac = jnp.where(same, base_or, fac)
-                    val = jnp.where(col < 2, fac, val)
+                        own = jnp.where((iota((CROWS, NB), 0) < NB) & keep, val, own)
+                    val = jnp.where(col < 2, own, val)
                 aflat[where, :] = val
-        store = pltpu.make_async_copy(a.at[part], out_ref.at[part], sems.at[5 + i])
+        store = pltpu.make_async_copy(
+            a.at[part, pl.ds(0, DEV)], out_ref.at[part], sems.at[CHUNKS + i]
+        )
         store.start()
         stores.append(store)
     for store in stores:
         store.wait()
 
 
-def update(table, inverses, work, new, old, panel, top, side):
-    n_old = old.shape[0]
+def update(table, work, new, old, g, fac, side):
     any_ = pl.BlockSpec(memory_space=pl.ANY)
+    vmem = pl.BlockSpec(memory_space=pltpu.VMEM)
     return pl.pallas_call(
-        functools.partial(update_kernel, n_old),
+        update_kernel,
         out_shape=jax.ShapeDtypeStruct((ROWS, DEV, NB), jnp.float32),
-        in_specs=[
-            pl.BlockSpec(memory_space=pltpu.SMEM),
-            pl.BlockSpec(memory_space=pltpu.VMEM),
-            pl.BlockSpec(memory_space=pltpu.VMEM),
-            any_, any_, any_, any_, any_, any_,
-        ],
+        in_specs=[pl.BlockSpec(memory_space=pltpu.SMEM), vmem, any_] + [vmem] * 5,
         out_specs=any_,
         scratch_shapes=[
-            pltpu.VMEM((ROWS, DEV, NB), jnp.float32),
-            pltpu.VMEM((NT + n_old, DEV, NB), jnp.float32),
-            pltpu.VMEM((2, ROWS, NB), jnp.float32),
-            pltpu.VMEM((2, NT + n_old, NB), jnp.float32),
-            pltpu.VMEM((NT, DEV * NB), jnp.bfloat16),
-            pltpu.VMEM((NT, DEV * NB), jnp.bfloat16),
-            pltpu.VMEM((ROWS, NT), jnp.bfloat16),
-            pltpu.VMEM((ROWS, NT), jnp.bfloat16),
-            pltpu.SemaphoreType.DMA((5 + CHUNKS,)),
+            pltpu.VMEM((ROWS, PITCH, NB), jnp.float32),
+            pltpu.VMEM((3 * NT, DEV * NB), jnp.bfloat16),
+            pltpu.VMEM((ROWS, 3 * NT), jnp.bfloat16),
+            pltpu.VMEM((ROWS, 2 * NB), jnp.float32),
+            pltpu.VMEM((ROWS, NB), jnp.float32),
+            pltpu.SemaphoreType.DMA((2 * CHUNKS,)),
         ],
         compiler_params=pltpu.CompilerParams(vmem_limit_bytes=40 * MIB),
-        name=f"update_{n_old}",
-    )(table, inverses, table, work, new, old, panel, top, side)
+        name="update",
+    )(table, table, work, new, old, g, fac, side)
 
 
 def on_device(matrix, pivots, block_inverses):
@@ -698,13 +676,14 @@
     table, send = plan(FEW, pivots, work)
 
     def few():
-        return update(table, block_inverses, work, *move(FEW, table, send, work))
+        return move(FEW, table, block_inverses, send, work)
 
     def many():
-        table, send = plan(MANY, pivots, work)
-        return update(table, block_inverses, work, *move(MANY, table, send, work))
-
-    out = lax.cond(table[T_MOST, 0] < FEW * DEV, few, many)
+        other, rows = plan(MANY, pivots, work)
+        return move(MANY, other, block_inverses, rows, work)
+
+    moved = lax.cond(table[T_OVER, 0] == 0, few, many)
+    out = update(table, work, *moved)
     return out.reshape(matrix.shape)
 
 

time: 72.9 us -> 65 us (0.89)
  the two profiles are of different devices: /device:TPU:97 before, /device:TPU:65 now
where the time goes in v3:
time: 65 us; the launch traced here: 64.7 us
  Pallas kernels  63.3 us (97%)
  between operations  0.85 us (1%)
    pallas_call x1, Pallas kernels, move(): pl.pallas_call(functools.partial(move_kernel, k), out_shape=tuple((jax.Sh...  47.3 us
    pallas_call x1, Pallas kernels, update(): pl.pallas_call(update_kernel, out_shape=jax.ShapeDtypeStruct((ROWS, DEV,...  11.2 us
    pallas_call x1, Pallas kernels, plan(): pl.pallas_call(functools.partial(plan_kernel, k), out_shape=(jax.ShapeDty...  4.84 us

profile of v3, /device:TPU:65, one launch (start us, length us, event | category | flops | bytes accessed | tf_op | source)
XLA Modules:
  0.0 64.7 jit_solution(16605253136581989871)
XLA Ops:
  0.0 0.0 copy-start.2
  0.0 0.0 copy-start.3
  0.0 4.8 %plan_2.1 = (s32[8,256]{1,0:T(8,128)S(1)}, f32[32,16,128]{2,1,0:T(8,128)S(1)}) custom-call(s32[2,128]{1,0:T(2,128)} %piv_ref.1, f32[1024,16,128]{2,1,0:T(8,128)} %bitcast.5), custom_call_target="tpu_custom_call" | custom-call | tf_op jit(solution)/shard_map/plan_2/pallas_call | solution.py:123
  4.9 0.5 slice.3
  6.0 0.0 copy-done.2
  6.0 0.0 copy-done.3
  6.0 47.3 %conditional.1 = ((f32[256,16,128]{2,1,0:T(8,128)S(1)}, f32[256,16,128]{2,1,0:T(8,128)}, f32[1024,256]{1,0:T(8,128)S(1)}, f32[1024,128]{1,0:T(8,128)}, f32[256,384]{1,0:T(8,128)})) conditional(s32[]{:T(128)} %bitcast.1, (s32[2,128]{1,0:T(2,128)S(1)}, f32[1024,16,128]{2,1,0:T(8,128)}, f32[2,128,128]{2,1,0:T(8,128)S(1)}) %tuple.21, ...), branch_computations={%region_0.0_spmd, %region_1.0_spmd} | conditional | bytes 8421440 | solution.py:685
  6.1 47.3 %move_2.1 = (f32[256,16,128]{2,1,0:T(8,128)S(1)}, f32[256,16,128]{2,1,0:T(8,128)}, f32[1024,256]{1,0:T(8,128)S(1)}, f32[1024,128]{1,0:T(8,128)}, f32[256,384]{1,0:T(8,128)}) custom-call(s32[8,256]{1,0:T(8,128)S(1)} %get-tuple-element.24.table_ref.place_ref, s32[8,256]{1,0:T(8,128)S(1)} %get-tuple-element.24.table_ref.place_ref, ...), custom_call_target="tpu_custom_call" | custom-call | tf_op jit(solution)/shard_map/cond/branch_1_fun/move_2/pallas_call | solution.py:541
  53.4 11.2 %update.1 = f32[1024,16,128]{2,1,0:T(8,128)} custom-call(s32[8,256]{1,0:T(8,128)S(1)} %get-tuple-element.35.table_ref.place_ref, s32[8,256]{1,0:T(8,128)S(1)} %get-tuple-element.35.table_ref.place_ref, f32[1024,16,128]{2,1,0:T(8,128)} %bitcast.8, f32[256,16,128]{2,1,0:T(8,128)S(1)} %get-tuple-element.37.new_ref, f32[256,16,128]{2,1,0:T(8,128)} %get-tuple-element.38.old_ref, ...), custom_call_target="tpu_custom_call" | custom-call | tf_op jit(solution)/shard_map/update/pallas_call | solution.py:656
Async XLA Ops:
  0.0 6.0 %copy-start.2 = (f32[2,128,128]{2,1,0:T(8,128)S(1)}, f32[2,128,128]{2,1,0:T(8,128)}, u32[]{:S(2)}) copy-start(f32[2,128,128]{2,1,0:T(8,128)} %param.7) | copy-start | bytes 393220
  0.0 6.0 %copy-start.3 = (s32[2,128]{1,0:T(2,128)S(1)}, s32[2,128]{1,0:T(2,128)}, u32[]{:S(2)}) copy-start(s32[2,128]{1,0:T(2,128)} %piv_ref.1) | copy-start | bytes 3076

commit v4 on v3

--- a/solution.py
+++ b/solution.py
@@ -29,7 +29,7 @@
     return iota(shape, dim).astype(jnp.float32)
 
 
-def plan_kernel(k, piv_ref, a_ref, table_ref, send_ref, row_buf, row_smem, sem, row_sem):
+def plan_kernel(k, piv_ref, a_ref, table_ref, send_ref, over_ref, row_buf, row_smem, sem, row_sem):
     me = lax.axis_index("prow")
     old = OLD[k]
     sq = (NT, NT)
@@ -64,10 +64,12 @@
     parent = jnp.max(jnp.where((t_col == lane) & before, sub, -1.0), axis=0, keepdims=True)
     c_row = jnp.where(parent < 0.0, lane1, parent)
 
-    def jump(_, c_row):
-        return down(sub == c_row, to_col(c_row))
-
-    c_row = lax.fori_loop(0, 8, jump, c_row)
+    def jump(carry):
+        _, c_row = carry
+        further = down(sub == c_row, to_col(c_row))
+        return jnp.max(jnp.abs(further - c_row)) > 0.5, further
+
+    _, c_row = lax.while_loop(lambda carry: carry[0], jump, (jnp.bool_(True), c_row))
 
     from_swap = down(sub == last_same, to_col(c_row))
     src = jnp.where(last_same < 0.0, t_row, from_swap).astype(jnp.int32)
@@ -105,7 +107,9 @@
     put(T_FIX, deal(mine, order, dst * NT + mid * DEV + turn))
     put(T_COUNT, jnp.sum(jnp.where(mine, 1.0, 0.0), axis=1, keepdims=True))
     over = (which >= k) | (goes & (turn >= old))
-    put(T_OVER, jnp.max(jnp.where(over, 1.0, 0.0), axis=1, keepdims=True))
+    any_over = jnp.max(jnp.where(over, 1.0, 0.0), axis=1, keepdims=True)
+    put(T_OVER, any_over)
+    over_ref[0, 0] = (jnp.max(any_over) > 0.5).astype(jnp.int32)
     put(7, jnp.zeros((1, 1), jnp.int32))
 
     to_smem.wait()
@@ -125,9 +129,14 @@
         out_shape=(
             jax.ShapeDtypeStruct((8, NT), jnp.int32),
             jax.ShapeDtypeStruct((DEV * k, DEV, NB), jnp.float32),
+            jax.ShapeDtypeStruct((1, 1), jnp.int32),
         ),
         in_specs=[pl.BlockSpec(memory_space=pltpu.VMEM), pl.BlockSpec(memory_space=pl.ANY)],
-        out_specs=(pl.BlockSpec(memory_space=pltpu.VMEM), pl.BlockSpec(memory_space=pl.ANY)),
+        out_specs=(
+            pl.BlockSpec(memory_space=pltpu.VMEM),
+            pl.BlockSpec(memory_space=pl.ANY),
+            pl.BlockSpec(memory_space=pltpu.SMEM),
+        ),
         scratch_shapes=[
             pltpu.VMEM((8, NT), jnp.int32),
             pltpu.SMEM((8, NT), jnp.int32),
@@ -151,13 +160,14 @@
     return dot(a[0], b[0]) + (dot(a[0], b[1]) + dot(a[1], b[0]))
 
 
-PIECES = 4
+X_FIRST = 10
+PIECES = 2
 
 
 def move_kernel(
     k, table_ref, place_ref, inv_ref, send_ref, a_ref,
-    new, old, g_ref, fac_ref, side_g,
-    got, mid, leave, leave2, first, panel, top, side,
+    b_hi, b_lo, g_hi, g_lo, fac_ref, old_out, side_out,
+    got, mid, leave, leave2, first, new, panel, top, side, old, side_g,
     s_got, r_got, s_out, r_out, s_mid, r_mid, s_ag, r_ag, s_z, r_z, s_sib, r_sib,
     s_top, r_top, s_far, r_far, s_loc,
 ):
@@ -232,45 +242,36 @@
     )
     own.start()
 
-    stage = jnp.where(core == 0, z, lax.rem(4 - z, 4))
-    onward = (me, jnp.where(core == 0, lax.rem(z + 1, 4), lax.rem(z + 3, 4)) * 2 + core)
     size = ROWS // PIECES
 
-    def z_part(i):
-        return panel.at[core, pl.ds(i * size, size)]
-
-    def z_onward(i):
-        return remote(z_part(i), z_part(i), s_z.at[i], r_z.at[i], onward)
-
-    def z_sibling(i):
-        return remote(z_part(i), z_part(i), s_sib.at[i], r_sib.at[i], sibling)
+    def z_part(which, i):
+        return panel.at[which, pl.ds(i * size, size)]
+
+    def z_out(i, j):
+        ref = z_part(core, i)
+        return remote(ref, ref, s_z.at[i, j], r_z.at[i], others[j])
+
+    def z_sibling(which, i):
+        ref = z_part(which, i)
+        return remote(ref, ref, s_sib.at[i], r_sib.at[i], sibling)
 
     def z_step(i):
         @pl.when(z > 0)
         def _():
-            z_onward(i).wait_recv()
-
-            @pl.when(stage < 3)
-            def _():
-                z_onward(i).start()
-
-            z_sibling(i).start()
+            z_out(i, 0).wait_recv()
+            z_sibling(core, i).start()
 
     def z_finish(i):
-        @pl.when(stage < 3)
-        def _():
-            z_onward(i).wait_send()
-
-        z_sibling(i).wait_send()
-        part = panel.at[1 - core, pl.ds(i * size, size)]
-        remote(part, part, s_sib.at[i], r_sib.at[i], sibling).wait_recv()
+        z_sibling(core, i).wait_send()
+        z_sibling(1 - core, i).wait_recv()
 
     @pl.when(is_root)
     def _():
         mine.wait()
         for i in range(PIECES):
-            z_onward(i).start()
-            z_sibling(i).start()
+            for j in range(3):
+                z_out(i, j).start()
+            z_sibling(core, i).start()
 
     def deal_out(half):
         return [
@@ -306,38 +307,47 @@
         return px * 4 + lax.rem(py + step + 4, 4)
 
     def part_of(index, half, part=None):
-        if part is None:
-            return new.at[pl.ds(index * 16, 16), pl.ds(half * 8, 8)]
-        return new.at[pl.ds(index * 16 + part * 8, 8), pl.ds(half * 8, 8)]
+        first_row, n = (0, X_FIRST) if half == 0 else (X_FIRST, 16 - X_FIRST)
+        if part is not None:
+            n = n // 2
+            first_row += part * n
+        return new.at[pl.ds(index * 16 + first_row, n)]
 
     class Gather:
         def __init__(self, half):
             self.half, self.base = half, half * 20
             self.axes = (0, 1) if half == 0 else (1, 0)
 
-        def copy(self, phase, item, role, index, part=None):
+        def copy(self, phase, item, role, index, part=None, step=None):
             n = self.base + phase * (1 + item) * 4 + role
             ref = part_of(index, self.half, part)
-            device = (ring(self.axes[phase], 1 if role % 2 == 0 else 3), col)
-            return remote(ref, ref, s_ag.at[n], r_ag.at[n], device)
-
-        def send(self, *args):
-            copy = self.copy(*args)
+            if step is None:
+                step = 1 if role % 2 == 0 else 3
+            return remote(ref, ref, s_ag.at[n], r_ag.at[n], (ring(self.axes[phase], step), col))
+
+        def send(self, *args, **kw):
+            copy = self.copy(*args, **kw)
             copy.start()
             sends.append(copy)
 
         def start(self, phase, item, index):
             for role in range(2):
                 self.send(phase, item, role, index)
+            if phase == 0:
+                self.send(phase, item, 2, index, step=2)
 
         def near(self, phase, item, index, role):
             came = shifted(index, self.axes[phase], 3 if role == 0 else 1)
             self.copy(phase, item, role, came).wait_recv()
-            self.send(phase, item, 2 + role, came, role)
+            if phase == 1:
+                self.send(phase, item, 2 + role, came, role)
             return came
 
         def far(self, phase, item, index):
             came = shifted(index, self.axes[phase], 2)
+            if phase == 0:
+                self.copy(phase, item, 2, came, step=2).wait_recv()
+                return came
             for role in range(2):
                 self.copy(phase, item, 2 + role, came, role).wait_recv()
             return came
@@ -346,6 +356,16 @@
     own.wait()
     for i in range(16):
         new[me * 16 + i] = got[table_ref[T_PICK, i]]
+    flat = new.reshape(NT * DEV, NB)
+
+    def convert(dx, dy):
+        index = at(x + dx, y + dy)[0]
+        rows = pl.ds(pl.multiple_of(index * 16, 16), 16)
+        for c in range(DEV):
+            hi, lo = split(flat[pl.ds(index * 16 * DEV + c, 16, stride=DEV), :])
+            b_hi[rows, c * NB : (c + 1) * NB] = hi
+            b_lo[rows, c * NB : (c + 1) * NB] = lo
+
     halves = [Gather(h) for h in range(2)]
     items = [[me], [me]]
     for g in halves:
@@ -381,13 +401,12 @@
         for j in range(len(plane)):
             top_send(j).start()
 
-    z_step(0)
+    convert(0, 0)
     for role in range(2):
         for h, g in enumerate(halves):
             came = g.near(0, 0, me, role)
             g.start(1, 1 + role, came)
             items[h].append(came)
-    z_step(1)
     for h, g in enumerate(halves):
         came = g.far(0, 0, me)
         g.start(1, 3, came)
@@ -412,8 +431,6 @@
     )
     own_old.start()
 
-    z_step(2)
-    z_step(3)
 
     @pl.when(is_root)
     def _():
@@ -431,6 +448,7 @@
             for role in range(2):
                 g.near(1, i, items[h][i], role)
 
+
     forward(0)
     forward(1)
 
@@ -441,12 +459,19 @@
 
     forward(2)
     forward(3)
+    for i in range(PIECES):
+        z_step(i)
     exchanged(leave2, old, both, s_mid, r_mid)
     own_old.wait()
+    outs = [
+        pltpu.make_async_copy(old, old_out.at[pl.ds(0, DEV * both)], s_loc.at[5]),
+        pltpu.make_async_copy(side_g, side_out.at[pl.ds(0, DEV * both)], s_loc.at[6]),
+    ]
+    outs[0].start()
 
     @pl.when(is_root)
     def _():
-        side[core] = old.reshape(N_OLD[MANY] * DEV, NB)[pl.ds(0, DEV * both, stride=DEV), :]
+        side[core] = old.reshape(DEV * both * DEV, NB)[pl.ds(0, DEV * both, stride=DEV), :]
         for i in range(3):
             spread(1, i).start()
         pass_on(1).start()
@@ -474,25 +499,33 @@
         l1 = dot3(split(p1 - dot3(split(l0), u0p)), inv[1])
         return l0, l0 - dot3(split(l1), l0b), l1
 
+    def placed(g0, l1):
+        return [
+            lax.dot_general(
+                val, order_t, (((1,), (1,)), ((), ())), preferred_element_type=jnp.float32
+            )
+            for val in split(jnp.concatenate([g0, l1], axis=1))
+        ]
+
+    def keep_factors(part, l0, g0, l1):
+        fac_ref[part, :] = jnp.where(col == 0, l0, l1)
+        for ref, val in zip((g_hi, g_lo), placed(g0, l1)):
+            ref[part, :] = val.astype(jnp.bfloat16)
+
     for i in range(4):
         part = pl.ds(i * 256, 256)
-        l0, g0, l1 = factors(panel[0, part, :], panel[1, part, :])
-        fac_ref[part, :] = l0
-        g_ref[part, 0:NB] = g0
-        g_ref[part, NB:] = l1
+        keep_factors(part, *factors(panel[0, part, :], panel[1, part, :]))
 
     unit = jnp.where(iota((NB, NB), 0) == iota((NB, NB), 1), -1.0, 0.0)
+    none = jnp.zeros((NB, NB), jnp.float32)
 
     @pl.when(me == 0)
     def _():
-        g_ref[0:NB, 0:NB] = unit
-        g_ref[0:NB, NB:] = jnp.zeros((NB, NB), jnp.float32)
+        keep_factors(pl.ds(0, NB), none, unit, none)
 
     @pl.when(me == 1)
     def _():
-        g_ref[0:NB, 0:NB] = l0b_full
-        g_ref[0:NB, NB:] = unit
-        fac_ref[0:NB, :] = l0b_full
+        keep_factors(pl.ds(0, NB), l0b_full, l0b_full, unit)
 
     @pl.when(z > 0)
     def _():
@@ -500,11 +533,20 @@
         pass_on(1).start()
 
     from_sibling(1).wait_recv()
-    for j, val in enumerate(factors(side[0], side[1])):
-        side_g[0 : DEV * both, j * NB : (j + 1) * NB] = val
+    l0, g0, l1 = factors(side[0], side[1])
+    for val, lanes in zip(placed(g0, l1), (slice(0, NT), slice(NT, 2 * NT))):
+        side_g[:, lanes] = val
+    side_g[:, 2 * NT :] = jnp.where(col == 0, l0, l1)
+    outs[1].start()
+    for dx, dy in offsets:
+        if dx != 2 and dy != 2:
+            convert(dx, dy)
     for i in range(4):
         for h, g in enumerate(halves):
             g.far(1, i, items[h][i])
+    for dx, dy in offsets:
+        if dx == 2 or dy == 2:
+            convert(dx, dy)
 
     for kind in range(2):
         pass_on(kind).wait_send()
@@ -514,6 +556,9 @@
         for kind in range(2):
             for i in range(3):
                 spread(kind, i).wait_send()
+        for i in range(PIECES):
+            for j in range(3):
+                z_out(i, j).wait_send()
         for j in range(len(plane)):
             top_send(j).wait_send()
 
@@ -526,32 +571,40 @@
 
     for copy in sends:
         copy.wait_send()
+    for copy in outs:
+        copy.wait()
 
 
 def move(k, table, inverses, send, work):
     both = OLD[k]
     dma = pltpu.SemaphoreType.DMA
-    outs = ((NT, DEV, NB), (N_OLD[MANY], DEV, NB), (ROWS, 2 * NB), (ROWS, NB), (N_OLD[MANY], 3 * NB))
+    f32, b16 = jnp.float32, jnp.bfloat16
+    outs = (
+        ((NT, DEV * NB), b16), ((NT, DEV * NB), b16),
+        ((ROWS, NT), b16), ((ROWS, NT), b16), ((ROWS, NB), f32),
+        ((N_OLD[MANY], DEV, NB), f32), ((N_OLD[MANY], 2 * NT + NB), f32),
+    )
     scratch = (
         (DEV * k, DEV, NB), (16, DEV, NB), (NB, DEV, NB), (DEV * both, DEV, NB), (NB, DEV, NB),
-        (2, ROWS, NB), (2, NT, NB), (2, DEV * both, NB),
+        (NT, DEV, NB), (2, ROWS, NB), (2, NT, NB), (2, DEV * both, NB), (DEV * both, DEV, NB),
+        (DEV * both, 2 * NT + NB),
     )
     any_ = pl.BlockSpec(memory_space=pl.ANY)
     vmem = pl.BlockSpec(memory_space=pltpu.VMEM)
     return pl.pallas_call(
         functools.partial(move_kernel, k),
-        out_shape=tuple(jax.ShapeDtypeStruct(s, jnp.float32) for s in outs),
+        out_shape=tuple(jax.ShapeDtypeStruct(*s) for s in outs),
         in_specs=[pl.BlockSpec(memory_space=pltpu.SMEM), vmem, vmem, any_, any_],
-        out_specs=(vmem,) * len(outs),
+        out_specs=(vmem,) * 5 + (pl.BlockSpec(memory_space=pltpu.HBM),) * 2,
         scratch_shapes=[pltpu.VMEM(s, jnp.float32) for s in scratch]
         + [
             dma((15,)), dma((15,)), dma((15,)), dma((2,)), dma((15,)), dma((15,)),
-            dma((40,)), dma((40,)), dma((PIECES,)), dma((PIECES,)),
+            dma((40,)), dma((40,)), dma((PIECES, 3)), dma((PIECES,)),
             dma((PIECES + 2,)), dma((PIECES + 2,)), dma((15,)), dma((15,)),
-            dma((2, 3)), dma((2,)), dma((5,)),
+            dma((2, 3)), dma((2,)), dma((7,)),
         ],
         compiler_params=pltpu.CompilerParams(
-            collective_id=k, has_side_effects=True, vmem_limit_bytes=32 * MIB
+            collective_id=k, has_side_effects=True, vmem_limit_bytes=(14 if k == FEW else 20) * MIB
         ),
         name=f"move_{k}",
     )(table, table, inverses, send, work)
@@ -563,19 +616,36 @@
 
 
 def update_kernel(
-    table_ref, place_ref, a_ref, new_ref, old_ref, g_ref, fac_ref, side_ref,
+    table_ref, a_ref, b_hi, b_lo, hi_ref, lo_ref, fac_ref, old_ref, side_ref,
     out_ref,
-    a, b3, g3, g, fac, sems,
+    a, g_hi, g_lo, fac, old, side, sems, old_sems,
 ):
     me = lax.axis_index("prow")
     col = lax.axis_index("pcol")
     few = table_ref[T_OVER, 0] == 0
     parts = [pl.ds(i * CROWS, CROWS) for i in range(CHUNKS)]
+
+    def old_loads(n):
+        part = pl.ds(0, n)
+        return [
+            pltpu.make_async_copy(old_ref.at[part], old.at[part], old_sems.at[0]),
+            pltpu.make_async_copy(side_ref.at[part], side.at[part], old_sems.at[1]),
+        ]
+
+    def each_old(do):
+        for cond, k in ((few, FEW), (jnp.logical_not(few), MANY)):
+
+            @pl.when(cond)
+            def _():
+                for copy in old_loads(N_OLD[k]):
+                    do(copy)
+
+    each_old(lambda copy: copy.start())
     loads = [
         pltpu.make_async_copy(a_ref.at[part], a.at[part, pl.ds(0, DEV)], sems.at[i])
         for i, part in enumerate(parts)
     ]
-    for copy in loads:
+    for copy in loads[:2]:
         copy.start()
 
     def each_fix(fix):
@@ -586,42 +656,31 @@
             packed = (src >> 4) * OLD[FEW] + (src & (DEV - 1))
             fix(entry >> 8, jnp.where(few, packed, src))
 
-    g[...] = g_ref[...]
+    aflat = a.reshape(ROWS * PITCH, NB)
+    g_hi[...] = hi_ref[...].astype(jnp.float32)
+    g_lo[...] = lo_ref[...].astype(jnp.float32)
     fac[...] = fac_ref[...]
 
     def fix_factors(dst, src):
-        row = side_ref[pl.ds(src, 1), :]
-        g[pl.ds(dst, 1), :] = row[:, NB:]
-        fac[pl.ds(dst, 1), :] = row[:, 0:NB]
-
+        row = side[pl.ds(src, 1), :]
+        g_hi[pl.ds(dst, 1), :] = row[:, :NT]
+        g_lo[pl.ds(dst, 1), :] = row[:, NT : 2 * NT]
+        fac[pl.ds(dst, 1), :] = row[:, 2 * NT :]
+
+    each_old(lambda copy: copy.wait())
     each_fix(fix_factors)
-
-    place = place_ref[T_PLACE : T_PLACE + 1, :]
-    order_t = jnp.where(iota((NT, NT), 0) == place, 1.0, 0.0).astype(jnp.bfloat16)
-    flat = new_ref.reshape(NT * DEV, NB)
-    for c in range(DEV):
-        hi, lo = split(flat[pl.ds(c, NT, stride=DEV), :])
-        for j, val in enumerate((hi, lo, hi)):
-            b3[j * NT : (j + 1) * NT, c * NB : (c + 1) * NB] = val
-    for part in parts:
-        g_hi, g_lo = (
-            lax.dot_general(
-                val, order_t, (((1,), (1,)), ((), ())), preferred_element_type=jnp.float32
-            ).astype(jnp.bfloat16)
-            for val in split(g[part, :])
-        )
-        for j, val in enumerate((g_hi, g_hi, g_lo)):
-            g3[part, j * NT : (j + 1) * NT] = val
-
-    aflat = a.reshape(ROWS * PITCH, NB)
     stores = []
     for i, part in enumerate(parts):
+        hi, lo = g_hi[part, :].astype(jnp.bfloat16), g_lo[part, :].astype(jnp.bfloat16)
+        left = jnp.concatenate([hi, hi, lo], axis=1)
         loads[i].wait()
+        if i + 2 < CHUNKS:
+            loads[i + 2].start()
 
         def fix_row(dst, src):
-            @pl.when((dst >> 8) == i)
+            @pl.when(dst // CROWS == i)
             def _():
-                a[dst, 0:DEV, :] = old_ref[src]
+                a[dst, 0:DEV, :] = old[src]
 
         each_fix(fix_row)
         if i == 0:
@@ -630,12 +689,14 @@
                 a[0:NB, 0:DEV, :] = jnp.zeros((NB, DEV, NB), jnp.float32)
 
         for c in range(0, DEV, 2):
-            upd = dot(g3[part, :], b3[:, c * NB : (c + 2) * NB])
+            wide = slice(c * NB, (c + 2) * NB)
+            right = jnp.concatenate([b_hi[:, wide], b_lo[:, wide], b_hi[:, wide]], axis=0)
+            upd = dot(left, right)
             for h in range(2):
                 where = pl.ds(i * CROWS * PITCH + c + h, CROWS, stride=PITCH)
                 val = aflat[where, :] - upd[:, h * NB : (h + 1) * NB]
                 if c + h == 0:
-                    own = jnp.where(col == 0, fac[part, :], g[part, NB:])
+                    own = fac[part, :]
                     if i == 0:
                         keep = jnp.where(col == 0, me == 0, me < 2)
                         own = jnp.where((iota((CROWS, NB), 0) < NB) & keep, val, own)
@@ -650,39 +711,41 @@
         store.wait()
 
 
-def update(table, work, new, old, g, fac, side):
+def update(table, work, *moved):
     any_ = pl.BlockSpec(memory_space=pl.ANY)
     vmem = pl.BlockSpec(memory_space=pltpu.VMEM)
     return pl.pallas_call(
         update_kernel,
         out_shape=jax.ShapeDtypeStruct((ROWS, DEV, NB), jnp.float32),
-        in_specs=[pl.BlockSpec(memory_space=pltpu.SMEM), vmem, any_] + [vmem] * 5,
+        in_specs=[pl.BlockSpec(memory_space=pltpu.SMEM), any_] + [vmem] * 5 + [pl.BlockSpec(memory_space=pltpu.HBM)] * 2,
         out_specs=any_,
         scratch_shapes=[
             pltpu.VMEM((ROWS, PITCH, NB), jnp.float32),
-            pltpu.VMEM((3 * NT, DEV * NB), jnp.bfloat16),
-            pltpu.VMEM((ROWS, 3 * NT), jnp.bfloat16),
-            pltpu.VMEM((ROWS, 2 * NB), jnp.float32),
+            pltpu.VMEM((ROWS, NT), jnp.float32),
+            pltpu.VMEM((ROWS, NT), jnp.float32),
             pltpu.VMEM((ROWS, NB), jnp.float32),
+            pltpu.VMEM((N_OLD[MANY], DEV, NB), jnp.float32),
+            pltpu.VMEM((N_OLD[MANY], 2 * NT + NB), jnp.float32),
             pltpu.SemaphoreType.DMA((2 * CHUNKS,)),
+            pltpu.SemaphoreType.DMA((2,)),
         ],
-        compiler_params=pltpu.CompilerParams(vmem_limit_bytes=40 * MIB),
+        compiler_params=pltpu.CompilerParams(vmem_limit_bytes=24 * MIB),
         name="update",
-    )(table, table, work, new, old, g, fac, side)
+    )(table, work, *moved)
 
 
 def on_device(matrix, pivots, block_inverses):
     work = matrix.reshape(ROWS, DEV, NB)
-    table, send = plan(FEW, pivots, work)
+    table, send, over = plan(FEW, pivots, work)
 
     def few():
         return move(FEW, table, block_inverses, send, work)
 
     def many():
-        other, rows = plan(MANY, pivots, work)
+        other, rows, _ = plan(MANY, pivots, work)
         return move(MANY, other, block_inverses, rows, work)
 
-    moved = lax.cond(table[T_OVER, 0] == 0, few, many)
+    moved = lax.cond(over.reshape(()) == 0, few, many)
     out = update(table, work, *moved)
     return out.reshape(matrix.shape)
 

time: 65 us -> 64.7 us (level)
  no operation moved by 1% of the time
where the time goes in v4:
time: 64.7 us; the launch traced here: 64 us
  Pallas kernels  62.9 us (97%)
  between operations  0.86 us (1%)
    pallas_call x1, Pallas kernels, move(): pl.pallas_call(functools.partial(move_kernel, k), out_shape=tuple((jax.Sh...  47.1 us
    pallas_call x1, Pallas kernels, update(): pl.pallas_call(update_kernel, out_shape=jax.ShapeDtypeStruct((ROWS, DEV,...  10.9 us
    pallas_call x1, Pallas kernels, plan(): pl.pallas_call(functools.partial(plan_kernel, k), out_shape=(jax.ShapeDty...  4.83 us

profile of v4, /device:TPU:65, one launch (start us, length us, event | category | flops | bytes accessed | tf_op | source)
XLA Modules:
  0.0 64.0 jit_solution(14902635370080951565)
XLA Ops:
  0.0 0.0 copy-start.2
  0.0 0.0 copy-start.3
  0.0 4.8 %plan_2.1 = (s32[8,256]{1,0:T(8,128)S(1)}, f32[32,16,128]{2,1,0:T(8,128)S(1)}, s32[1,1]{1,0:T(1,128)}) custom-call(s32[2,128]{1,0:T(2,128)} %piv_ref.1, f32[1024,16,128]{2,1,0:T(8,128)} %bitcast.5), custom_call_target="tpu_custom_call" | custom-call | tf_op jit(solution)/shard_map/plan_2/pallas_call | solution.py:127
  5.5 0.0 copy-done.2
  5.5 0.0 copy-done.3
  5.5 47.4 %conditional.1 = ((bf16[256,2048]{1,0:T(8,128)(2,1)S(1)}, bf16[256,2048]{1,0:T(8,128)(2,1)}, bf16[1024,256]{1,0:T(8,128)(2,1)}, bf16[1024,256]{1,0:T(8,128)(2,1)...) conditional(s32[]{:T(128)} %bitcast.1, (s32[2,128]{1,0:T(2,128)S(1)}, ...), branch_computations={%region_0.0_spmd, %region_1.0_spmd} | conditional | bytes 8421440 | solution.py:748
  5.5 47.1 %move_2.1 = (bf16[256,2048]{1,0:T(8,128)(2,1)S(1)}, bf16[256,2048]{1,0:T(8,128)(2,1)}, bf16[1024,256]{1,0:T(8,128)(2,1)}, bf16[1024,256]{1,0:T(8,128)(2,1)}, f32...) custom-call(s32[8,256]{1,0:T(8,128)S(1)} %get-tuple-element.24.table_ref.place_ref, ...), custom_call_target="tpu_custom_call" | custom-call | tf_op jit(solution)/shard_map/cond/branch_1_fun/move_2/pallas_call | solution.py:594
  52.9 10.9 %update.1 = f32[1024,16,128]{2,1,0:T(8,128)} custom-call(s32[8,256]{1,0:T(8,128)S(1)} %get-tuple-element.38.table_ref, f32[1024,16,128]{2,1,0:T(8,128)} %bitcast.8, bf16[256,2048]{1,0:T(8,128)(2,1)S(1)} %get-tuple-element.41.b_hi, bf16[256,2048]{1,0:T(8,128)(2,1)} %get-tuple-element.42.b_lo, bf16[1024,256]{1,0:T(8,128)(2,1)} %get-tuple-element.43.hi_ref, ...), custom_call_target="tpu_custom_call" | custom-call | tf_op jit(solution)/shard_map/update/pallas_call | solution.py:717
Async XLA Ops:
  0.0 5.5 %copy-start.2 = (f32[2,128,128]{2,1,0:T(8,128)S(1)}, f32[2,128,128]{2,1,0:T(8,128)}, u32[]{:S(2)}) copy-start(f32[2,128,128]{2,1,0:T(8,128)} %param.7) | copy-start | bytes 393220
  0.0 5.5 %copy-start.3 = (s32[2,128]{1,0:T(2,128)S(1)}, s32[2,128]{1,0:T(2,128)}, u32[]{:S(2)}) copy-start(s32[2,128]{1,0:T(2,128)} %piv_ref.1) | copy-start | bytes 3076

commit v5 on v4

--- a/solution.py
+++ b/solution.py
@@ -167,7 +167,7 @@
 def move_kernel(
     k, table_ref, place_ref, inv_ref, send_ref, a_ref,
     b_hi, b_lo, g_hi, g_lo, fac_ref, old_out, side_out,
-    got, mid, leave, leave2, first, new, panel, top, side, old, side_g,
+    got, mid, leave, leave2, first, wide, new, panel, top, side, old, side_g,
     s_got, r_got, s_out, r_out, s_mid, r_mid, s_ag, r_ag, s_z, r_z, s_sib, r_sib,
     s_top, r_top, s_far, r_far, s_loc,
 ):
@@ -194,7 +194,7 @@
     sibling = (me, z * 2 + 1 - core)
     others = [(me, lax.rem(z + i, 4) * 2 + core) for i in (1, 2, 3)]
 
-    mine = pltpu.make_async_copy(a_ref.at[:, 0, :], panel.at[core], s_loc.at[0])
+    mine = pltpu.make_async_copy(a_ref.at[:, pl.ds(0, 8)], wide, s_loc.at[0])
     block = pltpu.make_async_copy(a_ref.at[pl.ds(0, NB)], first, s_loc.at[1])
 
     @pl.when(is_root)
@@ -236,42 +236,43 @@
                 s_sem.at[j], r_sem.at[j], device,
             ).wait_recv()
 
+    size = ROWS // PIECES
+
+    def z_part(which, i):
+        return panel.at[which, pl.ds(i * size, size)]
+
+    def z_out(i, j):
+        ref = z_part(core, i)
+        return remote(ref, ref, s_z.at[i, j], r_z.at[i], others[j])
+
+    def z_sibling(which, i):
+        ref = z_part(which, i)
+        return remote(ref, ref, s_sib.at[i], r_sib.at[i], sibling)
+
+    def z_step(i):
+        @pl.when(z > 0)
+        def _():
+            z_out(i, 0).wait_recv()
+            z_sibling(core, i).start()
+
+    def z_finish(i):
+        z_sibling(core, i).wait_send()
+        z_sibling(1 - core, i).wait_recv()
+
+    @pl.when(is_root)
+    def _():
+        mine.wait()
+        panel[core] = wide.reshape(ROWS * 8, NB)[pl.ds(0, ROWS, stride=8), :]
+        for i in range(PIECES):
+            for j in range(3):
+                z_out(i, j).start()
+            z_sibling(core, i).start()
+
     exchange(send_ref, got, k, s_got, r_got)
     own = pltpu.make_async_copy(
         send_ref.at[pl.ds(me * k, k)], got.at[pl.ds(me * k, k)], s_loc.at[2]
     )
     own.start()
-
-    size = ROWS // PIECES
-
-    def z_part(which, i):
-        return panel.at[which, pl.ds(i * size, size)]
-
-    def z_out(i, j):
-        ref = z_part(core, i)
-        return remote(ref, ref, s_z.at[i, j], r_z.at[i], others[j])
-
-    def z_sibling(which, i):
-        ref = z_part(which, i)
-        return remote(ref, ref, s_sib.at[i], r_sib.at[i], sibling)
-
-    def z_step(i):
-        @pl.when(z > 0)
-        def _():
-            z_out(i, 0).wait_recv()
-            z_sibling(core, i).start()
-
-    def z_finish(i):
-        z_sibling(core, i).wait_send()
-        z_sibling(1 - core, i).wait_recv()
-
-    @pl.when(is_root)
-    def _():
-        mine.wait()
-        for i in range(PIECES):
-            for j in range(3):
-                z_out(i, j).start()
-            z_sibling(core, i).start()
 
     def deal_out(half):
         return [
@@ -586,7 +587,7 @@
     )
     scratch = (
         (DEV * k, DEV, NB), (16, DEV, NB), (NB, DEV, NB), (DEV * both, DEV, NB), (NB, DEV, NB),
-        (NT, DEV, NB), (2, ROWS, NB), (2, NT, NB), (2, DEV * both, NB), (DEV * both, DEV, NB),
+        (ROWS, 8, NB), (NT, DEV, NB), (2, ROWS, NB), (2, NT, NB), (2, DEV * both, NB), (DEV * both, DEV, NB),
         (DEV * both, 2 * NT + NB),
     )
     any_ = pl.BlockSpec(memory_space=pl.ANY)
@@ -604,7 +605,7 @@
             dma((2, 3)), dma((2,)), dma((7,)),
         ],
         compiler_params=pltpu.CompilerParams(
-            collective_id=k, has_side_effects=True, vmem_limit_bytes=(14 if k == FEW else 20) * MIB
+            collective_id=k, has_side_effects=True, vmem_limit_bytes=(18 if k == FEW else 24) * MIB
         ),
         name=f"move_{k}",
     )(table, table, inverses, send, work)

time: 64.7 us -> 64.8 us (level)
  no operation moved by 1% of the time
where the time goes in v5:
time: 64.8 us; the launch traced here: 64.5 us
  Pallas kernels  63.4 us (98%)
  between operations  0.86 us (1%)
    pallas_call x1, Pallas kernels, move(): pl.pallas_call(functools.partial(move_kernel, k), out_shape=tuple((jax.Sh...  47.4 us
    pallas_call x1, Pallas kernels, update(): pl.pallas_call(update_kernel, out_shape=jax.ShapeDtypeStruct((ROWS, DEV,...  11.5 us
    pallas_call x1, Pallas kernels, plan(): pl.pallas_call(functools.partial(plan_kernel, k), out_shape=(jax.ShapeDty...  4.55 us

profile of v5, /device:TPU:65, one launch (start us, length us, event | category | flops | bytes accessed | tf_op | source)
XLA Modules:
  0.0 64.5 jit_solution(1096067292439183370)
XLA Ops:
  0.0 0.0 copy-start.2
  0.0 0.0 copy-start.3
  0.0 4.6 %plan_2.1 = (s32[8,256]{1,0:T(8,128)S(1)}, f32[32,16,128]{2,1,0:T(8,128)S(1)}, s32[1,1]{1,0:T(1,128)}) custom-call(s32[2,128]{1,0:T(2,128)} %piv_ref.1, f32[1024,16,128]{2,1,0:T(8,128)} %bitcast.5), custom_call_target="tpu_custom_call" | custom-call | tf_op jit(solution)/shard_map/plan_2/pallas_call | solution.py:127
  5.2 0.0 copy-done.2
  5.2 0.0 copy-done.3
  5.2 47.6 %conditional.1 = ((bf16[256,2048]{1,0:T(8,128)(2,1)S(1)}, bf16[256,2048]{1,0:T(8,128)(2,1)}, bf16[1024,256]{1,0:T(8,128)(2,1)}, bf16[1024,256]{1,0:T(8,128)(2,1)...) conditional(s32[]{:T(128)} %bitcast.1, (s32[2,128]{1,0:T(2,128)S(1)}, ...), branch_computations={%region_0.0_spmd, %region_1.0_spmd} | conditional | bytes 8421440 | solution.py:749
  5.3 47.4 %move_2.1 = (bf16[256,2048]{1,0:T(8,128)(2,1)S(1)}, bf16[256,2048]{1,0:T(8,128)(2,1)}, bf16[1024,256]{1,0:T(8,128)(2,1)}, bf16[1024,256]{1,0:T(8,128)(2,1)}, f32...) custom-call(s32[8,256]{1,0:T(8,128)S(1)} %get-tuple-element.24.table_ref.place_ref, ...), custom_call_target="tpu_custom_call" | custom-call | tf_op jit(solution)/shard_map/cond/branch_1_fun/move_2/pallas_call | solution.py:595
  52.9 11.5 %update.1 = f32[1024,16,128]{2,1,0:T(8,128)} custom-call(s32[8,256]{1,0:T(8,128)S(1)} %get-tuple-element.38.table_ref, f32[1024,16,128]{2,1,0:T(8,128)} %bitcast.8, bf16[256,2048]{1,0:T(8,128)(2,1)S(1)} %get-tuple-element.41.b_hi, bf16[256,2048]{1,0:T(8,128)(2,1)} %get-tuple-element.42.b_lo, bf16[1024,256]{1,0:T(8,128)(2,1)} %get-tuple-element.43.hi_ref, ...), custom_call_target="tpu_custom_call" | custom-call | tf_op jit(solution)/shard_map/update/pallas_call | solution.py:718
Async XLA Ops:
  0.0 5.2 %copy-start.2 = (f32[2,128,128]{2,1,0:T(8,128)S(1)}, f32[2,128,128]{2,1,0:T(8,128)}, u32[]{:S(2)}) copy-start(f32[2,128,128]{2,1,0:T(8,128)} %param.7) | copy-start | bytes 393220
  0.0 5.2 %copy-start.3 = (s32[2,128]{1,0:T(2,128)S(1)}, s32[2,128]{1,0:T(2,128)}, u32[]{:S(2)}) copy-start(s32[2,128]{1,0:T(2,128)} %piv_ref.1) | copy-start | bytes 3076
